TPU v7x, 512 devices: a whole 4x8x8 slice. The times are simulated.
512 devices in a mesh: dp: 16 (over z, core), ctx: 4 (over x), enc: 8 (over y).
Axes of the slice: x: 4, y: 8, z: 8, core: 2. Of those that a mesh axis runs over, the one named last changes fastest.
Arguments:
- hidden: bfloat16 [16384, 4096], P(('dp', 'ctx')), may hold values from -16 to 16
- neighbour_states: bfloat16 [1536, 128, 896], P(('dp', 'ctx', 'enc')), may hold values from -16 to 16
- neighbour_owner: int32 [256, 2], P(('dp', 'ctx')), may hold values from 0 to 7, all different within a row; in each aligned block of 4 rows (0 to 3, 4 to 7, ...) at most 3 rows name the same one
- query_weight: bfloat16 [4096, 2048], P('dp', 'enc'), may hold values from -0.09375 to 0.09375
- key_weight: bfloat16 [896, 2048], P('dp', 'enc'), may hold values from -0.1875 to 0.1875
- value_weight: bfloat16 [896, 2048], P('dp', 'enc'), may hold values from -0.1875 to 0.1875
- out_weight: bfloat16 [2048, 4096], P('dp', 'enc'), may hold values from -0.5 to 0.5
- cotangent: bfloat16 [16384, 4096], P(('dp', 'ctx'), 'enc'), may hold values from -0.119628906 to 0.119628906
Outputs:
- mixed: bfloat16 [16384, 4096], P(('dp', 'ctx'), 'enc')
- grad_query_weight: float32 [4096, 2048], P('dp', 'enc')
Inputs may be any that keep to these rules, and one draw needn't show every extreme that they name: `neighbour_owner`: the 2 neighbours of a span lie at different owners; within the rows of one device (4 spans, aligned blocks) no owner is named more than 3 times.
All inputs are finite; a program needn't handle non-finite values.
Results may differ from a plain program's by a relative error of at most 0.024.
Values may be sent and summed in bfloat16 or wider, within the bound.
A program may use at most 64 MiB of HBM per device.

v0:
```python
import math

import jax
import jax.numpy as jnp
from jax import lax
from jax.sharding import Mesh
from jax.sharding import PartitionSpec as P

HEAD_DIM = 128
DP = ("dp_0", "dp_1")
DP_CTX = ("dp_0", "dp_1", "ctx")
DP_CTX_ENC = ("dp_0", "dp_1", "ctx", "enc")


def sent_to_all(value, axis):
    size = lax.axis_size(axis)
    return lax.all_to_all(
        jnp.broadcast_to(value[None], (size, *value.shape)), axis, 0, 0, tiled=True
    )


def joined_along(tiles, dim):
    lengths = list(tiles.shape[1:])
    lengths[dim] *= tiles.shape[0]
    return jnp.moveaxis(tiles, 0, dim).reshape(lengths)


def collect(value, axis, dim):
    tiles = sent_to_all(value, axis)
    return joined_along(tiles, dim)


def sent_together(arrays, axis, dim, along):
    both = jnp.concatenate(arrays, axis=along)
    filled, at, finished = (lax.all_gather(both, axis, axis=dim, tiled=True), 0, [])
    for a in arrays:
        finished.append(lax.slice_in_dim(filled, at, at + a.shape[along], axis=along))
        at += a.shape[along]
    return tuple(finished)


def passed_along(value, axis, by):
    size = lax.axis_size(axis)
    pairs = [(i, i + by) for i in range(size) if 0 <= i + by < size]
    return lax.ppermute(value, axis, pairs)


def cut_along(value, dim, size):
    lengths = value.shape
    tiles = value.reshape(*lengths[:dim], size, lengths[dim] // size, *lengths[dim + 1 :])
    return jnp.moveaxis(tiles, dim, 0)


def sum_at_owner(value, axis, dim):
    size = lax.axis_size(axis)
    tiles = lax.all_to_all(cut_along(value, dim, size), axis, 0, 0, tiled=True)
    return jnp.sum(tiles.astype(jnp.float32), axis=0)


def summed_rows(value, chips, core, dim):
    sizes = (lax.axis_size(chips), lax.axis_size(core))
    tiles = cut_along(value, dim, sizes[0] * sizes[1])
    inside = tiles.shape[1:]
    tiles = tiles.reshape(*sizes, *inside).swapaxes(0, 1).reshape(-1, *inside)
    tiles = lax.psum_scatter(tiles, core, scatter_dimension=0, tiled=True)
    return lax.psum_scatter(tiles, chips, scatter_dimension=0, tiled=True)[0]


def over_copies(value, axis):
    return sent_to_all(value, axis).sum(axis=0)


def slot_index(neighbour_owner, owner_count):
    flat_owner = neighbour_owner.reshape(-1)
    owner_ids = jnp.arange(owner_count, dtype=jnp.int32)
    onehot = (flat_owner[:, None] == owner_ids[None, :]).astype(jnp.int32)
    earlier = jnp.cumsum(onehot, axis=0) - onehot
    slot_rank = jnp.sum(earlier * onehot, axis=1)
    return (flat_owner, slot_rank)


def group_rows(matrix, span_len, head_count):
    width = matrix.shape[1]
    front_row = jnp.zeros((1, width), matrix.dtype)
    back_rows = jnp.zeros((span_len - 1, width), matrix.dtype)
    joined = jnp.concatenate([front_row, matrix, back_rows], axis=0)
    return joined.reshape(-1, span_len, head_count, HEAD_DIM)


def ungroup_rows(blocks, tok_rows):
    flat_rows = blocks.reshape(-1, blocks.shape[2] * blocks.shape[3])
    return flat_rows[1 : tok_rows + 1]


def shards(
    hidden,
    neighbour_states,
    neighbour_owner,
    query_weight,
    key_weight,
    value_weight,
    out_weight,
    cotangent,
):
    owner_count = lax.axis_size("enc")
    slot_count = neighbour_states.shape[0]
    span_count = neighbour_owner.shape[0]
    used_count = span_count * neighbour_owner.shape[1]
    tok_rows = hidden.shape[0]
    span_len = tok_rows // span_count
    local_proj = query_weight.shape[1]
    head_count = local_proj // HEAD_DIM
    inv_root = 1.0 / math.sqrt(HEAD_DIM)
    columns = hidden
    queries = jnp.dot(
        columns, collect(query_weight, DP, 0), preferred_element_type=jnp.float32
    ).astype(jnp.bfloat16)
    key_full, value_full = sent_together((key_weight, value_weight), DP, 0, 1)
    flat_owner, slot_rank = slot_index(neighbour_owner, owner_count)
    everyone = lax.all_gather(neighbour_states, "enc", axis=0, tiled=True)
    chosen = jnp.take(everyone, flat_owner * slot_count + slot_rank, axis=0)
    merged = chosen.reshape(used_count * chosen.shape[1], chosen.shape[2])
    keys = jnp.dot(merged, key_full, preferred_element_type=jnp.float32).astype(jnp.bfloat16)
    values = jnp.dot(merged, value_full, preferred_element_type=jnp.float32).astype(jnp.bfloat16)
    keys = keys.reshape(span_count, -1, local_proj)
    values = values.reshape(span_count, -1, local_proj)
    earlier_keys, earlier_values = passed_along((keys[-1], values[-1]), "ctx", 1)
    all_keys = jnp.concatenate([earlier_keys[None], keys], axis=0).reshape(
        span_count + 1, -1, head_count, HEAD_DIM
    )
    all_values = jnp.concatenate([earlier_values[None], values], axis=0).reshape(
        span_count + 1, -1, head_count, HEAD_DIM
    )
    grouped = group_rows(queries, span_len, head_count)
    scores = (
        jnp.einsum("cqhd,ckhd->chqk", grouped, all_keys, preferred_element_type=jnp.float32)
        * inv_root
    )
    probs = jax.nn.softmax(scores, axis=-1)
    blocks = jnp.einsum(
        "chqk,ckhd->cqhd",
        probs.astype(jnp.bfloat16),
        all_values,
        preferred_element_type=jnp.float32,
    )
    attention = ungroup_rows(blocks, tok_rows).astype(jnp.bfloat16)
    heads_all = collect(attention, "enc", 1)
    out_full = collect(out_weight, DP, 0)
    mixed = jnp.dot(heads_all, out_full, preferred_element_type=jnp.float32).astype(jnp.bfloat16)
    partial_grad = lax.dot_general(
        cotangent, out_full, (((1,), (1,)), ((), ())), preferred_element_type=jnp.float32
    )
    grad_attention = sum_at_owner(partial_grad.astype(jnp.bfloat16), "enc", 1).astype(jnp.bfloat16)
    grad_grouped = group_rows(grad_attention, span_len, head_count)
    grad_probs = jnp.einsum(
        "cqhd,ckhd->chqk", grad_grouped, all_values, preferred_element_type=jnp.float32
    )
    inner = jnp.sum(probs * grad_probs, axis=-1, keepdims=True)
    grad_scores = (probs * (grad_probs - inner)).astype(jnp.bfloat16)
    grad_blocks = (
        jnp.einsum("chqk,ckhd->cqhd", grad_scores, all_keys, preferred_element_type=jnp.float32)
        * inv_root
    )
    grad_queries = ungroup_rows(grad_blocks, tok_rows).astype(jnp.bfloat16)
    columns = hidden
    shard_grad = summed_rows(
        lax.dot_general(
            columns, grad_queries, (((0,), (0,)), ((), ())), preferred_element_type=jnp.float32
        ).astype(jnp.bfloat16),
        "dp_0",
        "dp_1",
        0,
    ).astype(jnp.float32)
    grad_query = over_copies(shard_grad, "ctx")
    return (mixed, grad_query)


def solution(mesh):
    torus = Mesh(
        mesh.devices.reshape(8, 2, mesh.shape["ctx"], mesh.shape["enc"]),
        ("dp_0", "dp_1", "ctx", "enc"),
    )
    in_specs = (
        P(DP_CTX, None),
        P(DP_CTX_ENC, None, None),
        P(DP_CTX, None),
        P(DP, "enc"),
        P(DP, "enc"),
        P(DP, "enc"),
        P(DP, "enc"),
        P(DP_CTX, "enc"),
    )
    out_specs = (P(DP_CTX, "enc"), P(DP, "enc"))
    return jax.shard_map(
        shards, mesh=torus, in_specs=in_specs, out_specs=out_specs, check_vma=False
    )
```

profile of v0, /device:TPU:24, one launch (start us, length us, event | category | flops | bytes accessed | tf_op | source)
XLA Modules:
  0.0 289.3 jit_solution(15542655225712940978)
XLA Ops:
  7.2 2.7 broadcast_in_dim.55
  9.8 10.6 %all-to-all-start.2 = ((bf16[16,128,512]{2,1,0:T(8,128)(2,1)}), bf16[16,128,512]{2,1,0:T(8,128)(2,1)}, u32[]{:S(2)}, u32[]{:S(2)}) async-start(bf16[16,128,512]{2,1,0:T(8,128)(2,1)} %broadcast_in_dim.55), calls=%async_computation.2 | async-start | bytes 4194304 | tf_op jit(solution)/shard_map/all_to_all | solution.py:17
  20.5 0.0 all-gather.2.cloned.1.call-start
  20.5 0.7 all-gather.2.cloned.1.call-update
  21.2 48.5 %all-to-all-done.2 = bf16[16,128,512]{2,1,0:T(8,128)(2,1)} async-done(((bf16[16,128,512]{2,1,0:T(8,128)(2,1)}), bf16[16,128,512]{2,1,0:T(8,128)(2,1)}, u32[]{:S(2)}, u32[]{:S(2)}) %all-to-all-start.2) | async-done | bytes 2097184 | tf_op jit(solution)/shard_map/all_to_all | solution.py:17
  69.7 1.5 broadcast_in_dim.53
  71.2 4.9 %all-to-all-start = ((bf16[16,256,256]{2,1,0:T(8,128)(2,1)}), bf16[16,256,256]{2,1,0:T(8,128)(2,1)}, u32[]{:S(2)}, u32[]{:S(2)}) async-start(bf16[16,256,256]{2,1,0:T(8,128)(2,1)} %broadcast_in_dim.53), calls=%async_computation | async-start | bytes 4194304 | tf_op jit(solution)/shard_map/all_to_all | solution.py:17
  76.2 0.1 copy.42
  76.2 0.1 reshape.97
  76.3 0.1 fusion.15
  76.4 2.3 convolution_convert_fusion.1
  78.8 1.1 copy.71
  79.8 45.5 %all-to-all-done = bf16[16,256,256]{2,1,0:T(8,128)(2,1)} async-done(((bf16[16,256,256]{2,1,0:T(8,128)(2,1)}), bf16[16,256,256]{2,1,0:T(8,128)(2,1)}, u32[]{:S(2)}, u32[]{:S(2)}) %all-to-all-start) | async-done | bytes 2097184 | tf_op jit(solution)/shard_map/all_to_all | solution.py:17
  125.4 7.3 %all-to-all-start.3 = ((bf16[8,256,256]{2,1,0:T(8,128)(2,1)}), bf16[8,256,256]{2,1,0:T(8,128)(2,1)S(1)}, u32[]{:S(2)}, u32[]{:S(2)}) async-start(bf16[8,256,256]{2,1,0:T(8,128)(2,1)} %bitcast.60), calls=%async_computation.3 | async-start | bytes 2097152 | tf_op jit(solution)/shard_map/all_to_all | solution.py:56
  132.7 0.1 copy.43
  132.8 0.1 mul.44
  132.9 0.1 pad.7.clone
  133.0 0.2 select_reduce_fusion
  133.3 0.1 broadcast_bitcast_fusion
  133.3 19.6 %all_gather.7 = bf16[896,512]{1,0:T(8,128)(2,1)} all-gather(bf16[56,512]{1,0:T(8,128)(2,1)S(1)} %pad_maximum_fusion), channel_id=1, replica_groups=mesh['dp_0'=8,'dp_1'=2,'ctx'=4,'enc'=8] {'dp_0','dp_1'}, dimensions={0}, use_global_device_ids=true | all-gather | bytes 974848 | tf_op jit(solution)/shard_map/all_gather | solution.py:35
  152.9 2.3 convolution_convert_fusion.6
  155.2 2.1 all-to-all-done.3
  157.3 0.1 reduce_sum.53
  157.5 0.2 maximum_maximum_fusion.1
  157.6 0.7 reshape.104
  158.4 4.6 %gather_fusion = bf16[8,128,896]{2,1,0:T(8,128)(2,1)} fusion(bf16[24,128,896]{2,1,0:T(8,128)(2,1)} %all-gather.2.cloned.1.call-done, s32[1024]{0:T(1024)S(1)} %pad_clamp_fusion), kind=kCustom, calls=%fused_computation | custom fusion | bytes 3670048 | tf_op jit(solution)/shard_map/jit(_take)/gather | solution.py:121
  163.0 1.9 bitcast_select_fusion
  164.9 0.7 convolution_convert_fusion.3
  165.7 4.1 %collective-permute-start = (bf16[256,256]{1,0:T(8,128)(2,1)S(1)}, bf16[256,256]{1,0:T(8,128)(2,1)}, u32[]{:S(2)}, u32[]{:S(2)}) collective-permute-start(bf16[256,256]{1,0:T(8,128)(2,1)S(1)} %slice.33), channel_id=1, source_target_pairs={{0,8},{8,16},{16,24},{1,9},{9,17},{17,25},{2,10},{10,18},{18,26},{... | collective-permute-start | bytes 393224 | tf_op jit(solution)/shard_map/ppermute | solution.py:45
  169.7 1.5 convolution_convert_fusion.2
  171.2 0.1 concatenate.27
  171.4 1.6 slice.31
  172.9 1.2 concatenate.31
  174.1 3.4 %collective-permute-start.1 = (bf16[256,256]{1,0:T(8,128)(2,1)}, bf16[256,256]{1,0:T(8,128)(2,1)}, u32[]{:S(2)}, u32[]{:S(2)}) collective-permute-start(bf16[256,256]{1,0:T(8,128)(2,1)} %slice.31), channel_id=1, source_target_pairs={{0,8},{8,16},{16,24},{1,9},{9,17},{17,25},{2,10},{10,18},{18,26},{... | collective-permute-start | bytes 393224 | tf_op jit(solution)/shard_map/ppermute | solution.py:45
  177.5 0.9 concatenate.26
  178.5 0.7 copy_dynamic-update-slice_fusion.3
  179.1 0.6 collective-permute-done.1
  179.7 0.9 concatenate.30
  180.7 0.1 copy_dynamic-update-slice_fusion
  180.8 0.4 convolution_multiply_fusion
  181.2 1.7 fusion.17
  182.9 0.1 copy_dynamic-update-slice_fusion.1
  183.1 1.2 multiply_reduce_fusion
  184.3 0.2 copy-done.3
  184.5 3.1 %fusion.6 = bf16[5,64,2,128]{3,1,2,0:T(8,128)(2,1)} fusion(bf16[5,256,2,128]{3,1,2,0:T(8,128)(2,1)S(1)} %copy-done.3, f32[5,2,64,256]{3,2,1,0:T(8,128)} %get-tuple-element.7, f32[5,2,64]{2,1,0:T(2,128)S(1)} %get-tuple-element.6, f32[5,2,64]{2,1,0:T(2,128)S(1)} %get-tuple-element.4, f32[5,2,64,256]{3,2,1,0:T(8,128)S(1)} %convolution_multiply_fusion), kind=kOutput, calls=%fused_computation.17 | convolution fusion | flops 42926976 | bytes 2135040 | tf_op jit(solution)/shard_map/chqk,ckhd->cqhd/dot_general | solution.py:161
  187.6 1.1 copy.53
  188.7 2.0 fusion.1
  190.7 4.5 %reshape_reshape.3 = bf16[8,2,256,256]{2,1,0,3:T(2,128)(2,1)} reshape(bf16[4096,256]{0,1:T(8,128)(2,1)} %fusion.1) | data formatting | bytes 4194304 | tf_op jit(solution)/shard_map/reshape;reshape | solution.py:64
  195.2 6.1 %copy.54 = bf16[8,2,256,256]{3,2,0,1:T(8,128)(2,1)} copy(bf16[8,2,256,256]{2,1,0,3:T(2,128)(2,1)} %reshape_reshape.3) | data formatting | bytes 4194304 | tf_op jit(solution)/shard_map/reshape;reshape | solution.py:64
  201.3 0.0 reduce-scatter.5.cloned.1.call-start
  201.4 16.5 %reduce-scatter.3.cloned.1.call-done = bf16[8,256,256]{2,1,0:T(8,128)(2,1)} async-done(((bf16[16,256,256]{2,1,0:T(8,128)(2,1)}), bf16[8,256,256]{2,1,0:T(8,128)(2,1)}) %reduce-scatter.3.cloned.1.call-update) | async-done | bytes 1048592 | tf_op jit(solution)/shard_map/reduce_scatter | solution.py:65
  217.9 2.3 fusion.5
  220.2 0.2 copy.49
  220.5 0.1 copy.50
  220.6 1.0 broadcast_in_dim.54
  221.6 7.2 %all-to-all-start.1 = ((bf16[8,256,256]{1,2,0:T(8,128)(2,1)}), bf16[8,256,256]{1,2,0:T(8,128)(2,1)S(1)}, u32[]{:S(2)}, u32[]{:S(2)}) async-start(bf16[8,256,256]{1,2,0:T(8,128)(2,1)} %broadcast_in_dim.54), calls=%async_computation.1 | async-start | bytes 2097152 | tf_op jit(solution)/shard_map/all_to_all | solution.py:17
  228.8 35.6 %reduce-scatter.5.cloned.1.call-done = bf16[1,256,256]{2,1,0:T(8,128)(2,1)} async-done(((bf16[8,256,256]{2,1,0:T(8,128)(2,1)}), bf16[1,256,256]{2,1,0:T(8,128)(2,1)}) %reduce-scatter.5.cloned.1.call-update) | async-done | bytes 131088 | tf_op jit(solution)/shard_map/reduce_scatter | solution.py:66
  264.5 0.9 bitcast_convert_fusion
  265.4 1.2 broadcast_in_dim.58
  266.6 0.1 copy-done.1
  266.7 4.3 %all-to-all-start.4 = ((f32[4,256,256]{2,1,0:T(8,128)}), f32[4,256,256]{2,1,0:T(8,128)S(1)}, u32[]{:S(2)}, u32[]{:S(2)}) async-start(f32[4,256,256]{2,1,0:T(8,128)} %broadcast_in_dim.58), calls=%async_computation.6 | async-start | bytes 2097152 | tf_op jit(solution)/shard_map/all_to_all | solution.py:17
  271.0 3.3 %convolution_convert_fusion.4 = bf16[256,512]{1,0:T(8,128)(2,1)} fusion(bf16[256,2048]{0,1:T(8,128)(2,1)} %bitcast.65, bf16[2048,512]{1,0:T(8,128)(2,1)} %bitcast.8), kind=kOutput, calls=%fused_computation.11 | convolution fusion | flops 537001984 | bytes 3407872 | tf_op jit(solution)/shard_map/dot_general | solution.py:149
  274.4 7.7 %all-to-all-done.4 = f32[4,256,256]{2,1,0:T(8,128)S(1)} async-done(((f32[4,256,256]{2,1,0:T(8,128)}), f32[4,256,256]{2,1,0:T(8,128)S(1)}, u32[]{:S(2)}, u32[]{:S(2)}) %all-to-all-start.4) | async-done | bytes 1048608 | tf_op jit(solution)/shard_map/all_to_all | solution.py:17
  282.0 0.8 reduce_sum.55
  (44 shorter events, 0.3 us)
Async XLA Ops:
  7.2 145.7 %copy-start = (bf16[256,4096]{1,0:T(8,128)(2,1)S(1)}, bf16[256,4096]{1,0:T(8,128)(2,1)}, u32[]{:S(2)}) copy-start(bf16[256,4096]{1,0:T(8,128)(2,1)} %param.8) | copy-start | bytes 6291460
  9.8 59.8 %copy-start.7 = (bf16[256,256]{1,0:T(8,128)(2,1)S(1)}, bf16[256,256]{1,0:T(8,128)(2,1)}, u32[]{:S(2)}) copy-start(bf16[256,256]{1,0:T(8,128)(2,1)} %param.11) | copy-start | bytes 393220
  9.8 59.8 %all-to-all-start.2 = ((bf16[16,128,512]{2,1,0:T(8,128)(2,1)}), bf16[16,128,512]{2,1,0:T(8,128)(2,1)}, u32[]{:S(2)}, u32[]{:S(2)}) async-start(bf16[16,128,512]{2,1,0:T(8,128)(2,1)} %broadcast_in_dim.55), calls=%async_computation.2 | async-start | bytes 4194304 | tf_op jit(solution)/shard_map/all_to_all | solution.py:17
  20.5 138.0 %all-gather.2.cloned.1.call-start = ((), (), s32[]{:S(2)}) async-start(), calls=%async_computation.7 | async-start | bytes 6193152 | tf_op jit(solution)/shard_map/all_gather | solution.py:120
  71.2 4.9 %copy-start.12 = (s32[4,2]{0,1:T(2,128)S(1)}, s32[4,2]{0,1:T(2,128)}, u32[]{:S(2)}) copy-start(s32[4,2]{0,1:T(2,128)} %param.10) | copy-start | bytes 100
  71.2 5.2 %copy-start.5 = (bf16[256,512]{1,0:T(8,128)(2,1)S(1)}, bf16[256,512]{1,0:T(8,128)(2,1)}, u32[]{:S(2)}) copy-start(bf16[256,512]{1,0:T(8,128)(2,1)} %param.15) | copy-start | bytes 786436
  71.2 54.2 %all-to-all-start = ((bf16[16,256,256]{2,1,0:T(8,128)(2,1)}), bf16[16,256,256]{2,1,0:T(8,128)(2,1)}, u32[]{:S(2)}, u32[]{:S(2)}) async-start(bf16[16,256,256]{2,1,0:T(8,128)(2,1)} %broadcast_in_dim.53), calls=%async_computation | async-start | bytes 4194304 | tf_op jit(solution)/shard_map/all_to_all | solution.py:17
  78.8 54.5 %copy-start.8 = (bf16[56,256]{1,0:T(8,128)(2,1)S(1)}, bf16[56,256]{1,0:T(8,128)(2,1)}, u32[]{:S(2)}) copy-start(bf16[56,256]{1,0:T(8,128)(2,1)} %param.13) | copy-start | bytes 86020
  78.8 54.5 %copy-start.9 = (bf16[56,256]{1,0:T(8,128)(2,1)S(1)}, bf16[56,256]{1,0:T(8,128)(2,1)}, u32[]{:S(2)}) copy-start(bf16[56,256]{1,0:T(8,128)(2,1)} %param.12) | copy-start | bytes 86020
  125.4 31.9 %all-to-all-start.3 = ((bf16[8,256,256]{2,1,0:T(8,128)(2,1)}), bf16[8,256,256]{2,1,0:T(8,128)(2,1)S(1)}, u32[]{:S(2)}, u32[]{:S(2)}) async-start(bf16[8,256,256]{2,1,0:T(8,128)(2,1)} %bitcast.60), calls=%async_computation.3 | async-start | bytes 2097152 | tf_op jit(solution)/shard_map/all_to_all | solution.py:56
  132.7 85.2 %reduce-scatter.3.cloned.1.call-start = ((), (), s32[]{:S(2)}) async-start(), calls=%async_computation.8 | async-start | bytes 3145728 | tf_op jit(solution)/shard_map/reduce_scatter | solution.py:65
  163.0 1.9 copy-start.4
  165.7 11.8 %collective-permute-start = (bf16[256,256]{1,0:T(8,128)(2,1)S(1)}, bf16[256,256]{1,0:T(8,128)(2,1)}, u32[]{:S(2)}, u32[]{:S(2)}) collective-permute-start(bf16[256,256]{1,0:T(8,128)(2,1)S(1)} %slice.33), channel_id=1, source_target_pairs={{0,8},{8,16},{16,24},{1,9},{9,17},{17,25},{2,10},{10,18},{18,26},{... | collective-permute-start | bytes 393224 | tf_op jit(solution)/shard_map/ppermute | solution.py:45
  174.1 5.6 %collective-permute-start.1 = (bf16[256,256]{1,0:T(8,128)(2,1)}, bf16[256,256]{1,0:T(8,128)(2,1)}, u32[]{:S(2)}, u32[]{:S(2)}) collective-permute-start(bf16[256,256]{1,0:T(8,128)(2,1)} %slice.31), channel_id=1, source_target_pairs={{0,8},{8,16},{16,24},{1,9},{9,17},{17,25},{2,10},{10,18},{18,26},{... | collective-permute-start | bytes 393224 | tf_op jit(solution)/shard_map/ppermute | solution.py:45
  180.6 2.3 copy-start.10
  180.8 2.3 copy-start.2
  180.8 2.3 copy-start.6
  183.1 1.2 copy-start.11
  183.1 1.4 copy-start.3
  201.3 63.1 %reduce-scatter.5.cloned.1.call-start = ((), (), s32[]{:S(2)}) async-start(), calls=%async_computation.9 | async-start | bytes 1179648 | tf_op jit(solution)/shard_map/reduce_scatter | solution.py:66
  221.6 43.8 %all-to-all-start.1 = ((bf16[8,256,256]{1,2,0:T(8,128)(2,1)}), bf16[8,256,256]{1,2,0:T(8,128)(2,1)S(1)}, u32[]{:S(2)}, u32[]{:S(2)}) async-start(bf16[8,256,256]{1,2,0:T(8,128)(2,1)} %broadcast_in_dim.54), calls=%async_computation.1 | async-start | bytes 2097152 | tf_op jit(solution)/shard_map/all_to_all | solution.py:17
  265.4 1.3 copy-start.1
  266.7 15.3 %all-to-all-start.4 = ((f32[4,256,256]{2,1,0:T(8,128)}), f32[4,256,256]{2,1,0:T(8,128)S(1)}, u32[]{:S(2)}, u32[]{:S(2)}) async-start(f32[4,256,256]{2,1,0:T(8,128)} %broadcast_in_dim.58), calls=%async_computation.6 | async-start | bytes 2097152 | tf_op jit(solution)/shard_map/all_to_all | solution.py:17
Sparse Core Ops, SparseCore 0:
  23.4 70.3 all-gather.1
  201.5 16.4 reduce-scatter.2
  221.0 43.4 reduce-scatter.4
where the time goes:
time: 290 us; the launch traced here: 289 us
  waiting for transfers between devices  157 us (54%)
  starting transfers between devices  41.9 us (14%)
  local copies, waits for them, and re-layouts  31.5 us (11%)
  blocking collectives  19.6 us (7%)
  matrix products  19.1 us (7%)
  between operations  14.1 us (5%)
  other arithmetic  5.94 us (2%)
    all_to_all x4, waiting for transfers between devices, sent_to_all(): lax.all_to_all(jnp.broadcast_to(value[None], (size, *value.shape)), axis,...  102 us
    reduce_scatter x1, waiting for transfers between devices, summed_rows(): return lax.psum_scatter(tiles, chips, scatter_dimension=0, tiled=True)[0]  35.6 us
    all_to_all x4, starting transfers between devices, sent_to_all(): lax.all_to_all(jnp.broadcast_to(value[None], (size, *value.shape)), axis,...  27.1 us
    all_gather x1, blocking collectives, sent_together(): lax.all_gather(both, axis, axis=dim, tiled=True)  19.6 us
    reduce_scatter x1, waiting for transfers between devices, summed_rows(): tiles = lax.psum_scatter(tiles, core, scatter_dimension=0, tiled=True)  16.5 us
    another operation x2, local copies, waits for them, and re-layouts, summed_rows(): tiles = tiles.reshape(*sizes, *inside).swapaxes(0, 1).reshape(-1, *inside)  10.6 us
    ppermute x2, starting transfers between devices, passed_along(): return lax.ppermute(value, axis, pairs)  7.46 us
    all_to_all x1, starting transfers between devices, sum_at_owner(): tiles = lax.all_to_all(cut_along(value, dim, size), axis, 0, 0, tiled=True)  7.32 us
  transfers between devices with their start and end apart: 10, of which 7 were waited for; matrix products, arithmetic and copies ran while one was open for 8% of the time, Pallas kernels for 0%

commit v1 on v0

v1 whole, which is shorter than its diff:
```python
import functools
import math

import jax
import jax.numpy as jnp
from jax import lax
from jax.experimental import pallas as pl
from jax.experimental.pallas import tpu as pltpu
from jax.sharding import PartitionSpec as P

HEAD_DIM = 128
MESH = pl.DeviceIdType.MESH
BF16 = jnp.bfloat16
F32 = jnp.float32
NT = (((1,), (1,)), ((), ()))


def dot(a, b, dims=(((1,), (0,)), ((), ()))):
    return lax.dot_general(a, b, dims, preferred_element_type=F32)


def rows_of(ref, index, count):
    step = 128 if count % 128 == 0 else 16
    return ref.at[pl.ds(pl.multiple_of(index * count, step), count)]


class Ring:
    def __init__(self, buf, slot, first, send, recv, right, left, own=None):
        self.buf, self.slot = buf, slot
        self.first, self.send, self.recv = first, send, recv
        self.right, self.left, self.own = right, left, own
        self.sent = []

    def part(self, ref, half):
        if half == 0:
            return ref.at[pl.ds(0, self.first)]
        return ref.at[pl.ds(self.first, ref.shape[0] - self.first)]

    def start(self, step, last):
        for way, to, sign in ((0, self.right, -1), (1, self.left, 1)):
            dst = self.slot(sign * (step - 1))
            src = self.own if step == 1 and self.own is not None else dst
            if step == last:
                src, dst = self.part(src, way), self.part(dst, way)
            copy = pltpu.make_async_remote_copy(
                src_ref=src,
                dst_ref=dst,
                send_sem=self.send.at[way, step - 1],
                recv_sem=self.recv.at[way, step - 1],
                device_id=to,
                device_id_type=MESH,
            )
            copy.start()
            self.sent.append(copy)

    def wait(self, step, last):
        for way, sign in ((0, -1), (1, 1)):
            dst = self.slot(sign * step)
            if step == last:
                dst = self.part(dst, way)
            pltpu.make_async_remote_copy(
                src_ref=dst,
                dst_ref=dst,
                send_sem=self.send.at[way, step - 1],
                recv_sem=self.recv.at[way, step - 1],
                device_id=self.right,
                device_id_type=MESH,
            ).wait_recv()


def kernel(
    cores, nz, nx, ny, spans, hid_h, st_h, owner, wq_h, wk_v, wv_v, wo_h, cot_h, mixed_o, grad_o,
    hid, cot, wq, wo, wkv, kvw_f, kvw, a2a, picked, kv, gpart, rs_out, rs_in, qpad, gpad, probs,
    apad, att, gqpad, gqt, sib_out, sib_in, xs, x_in, zs, z_in, fin, acc,
    local_sem, a2a_s, a2a_r, pick_s, pick_r, rs_s, rs_r, att_s, att_r,
    wo_s, wo_r, wq_s, wq_r, kw_s, kw_r, wo_cs, wo_cr, wq_cs, wq_cr, kw_cs, kw_cr,
    halo_s, halo_r, sib_s, sib_r, x_s, x_r, z_s, z_r, f_s, f_r,
):
    dp, x, y = lax.axis_index("dp"), lax.axis_index("ctx"), lax.axis_index("enc")
    z, core = lax.div(dp, cores), lax.rem(dp, cores)
    sib = {"dp": z * cores + (1 - core)}

    def zat(k):
        return lax.rem(z + (k + nz), nz)

    def xat(k):
        return lax.rem(x + (k + nx), nx)

    def yat(k):
        return lax.rem(y + (k + ny), ny)

    def zdev(k):
        return {"dp": zat(k) * cores + core}

    def xdev(k):
        return {"ctx": xat(k)}

    def ydev(k):
        return {"enc": yat(k)}

    hy, hz = ny // 2, nz // 2
    tok = hid.shape[0]
    proj = wq.shape[1]
    heads = proj // HEAD_DIM
    span = tok // spans
    pairs = picked.shape[1]
    used = owner.shape[0] * owner.shape[1]
    piece = pairs // used
    scale = 1.0 / math.sqrt(HEAD_DIM)
    sent = []

    def remote(src, dst, s, r, to, start=True):
        copy = pltpu.make_async_remote_copy(
            src_ref=src, dst_ref=dst, send_sem=s, recv_sem=r, device_id=to, device_id_type=MESH
        )
        if start:
            copy.start()
            sent.append(copy)
        return copy

    with jax.named_scope("entry"):
        barrier = pltpu.get_barrier_semaphore()
        peers = [sib]
        peers += [ydev(k) for k in range(1, ny)]
        peers += [xdev(k) for k in range(1, nx)]
        peers += [zdev(k) for k in range(1, nz)]
        for peer in peers:
            pl.semaphore_signal(barrier, inc=1, device_id=peer, device_id_type=MESH)

        local = [
            pltpu.make_async_copy(st_h.at[:, pl.ds(pl.multiple_of(y * piece, 16), piece), :], a2a.at[y], local_sem.at[0]),
            pltpu.make_async_copy(wo_h, rows_of(wo, dp, wo_h.shape[0]), local_sem.at[1]),
            pltpu.make_async_copy(wq_h, rows_of(wq, dp, wq_h.shape[0]), local_sem.at[2]),
            pltpu.make_async_copy(cot_h, cot, local_sem.at[3]),
            pltpu.make_async_copy(hid_h, hid, local_sem.at[4]),
        ]
        for copy in local:
            copy.start()
        kw_rows = wk_v.shape[0]
        rows_of(wkv, dp, 2 * kw_rows)[...] = jnp.concatenate(
            [wk_v[...].astype(F32), wv_v[...].astype(F32)], axis=0
        ).astype(BF16)
        qpad[...] = jnp.zeros_like(qpad)
        gpad[...] = jnp.zeros_like(gpad)
        pl.semaphore_wait(barrier, len(peers))

    def weight_ring(buf, own, first, s, r):
        rows = buf.shape[0] // (cores * nz)
        return Ring(buf, lambda k: rows_of(buf, zat(k) * cores + core, rows), first, s, r, zdev(1), zdev(-1), own)

    wo_ring = weight_ring(wo, wo_h, wo_h.shape[0] // 2, wo_s, wo_r)
    wq_ring = weight_ring(wq, wq_h, wq_h.shape[0] // 2, wq_s, wq_r)
    kw_ring = weight_ring(wkv, None, 64, kw_s, kw_r)
    weights = ((wo_ring, wo_cs, wo_cr), (kw_ring, kw_cs, kw_cr), (wq_ring, wq_cs, wq_cr))

    def pass_on(k):
        for ring, s, r in weights:
            block = ring.slot(k)
            src = ring.own if k == 0 and ring.own is not None else block
            remote(src, block, s.at[k % nz], r.at[k % nz], sib)

    def from_sibling(ring, s, r, buf):
        rows = buf.shape[0] // (cores * nz)
        for k in range(nz):
            block = rows_of(buf, zat(k) * cores + (1 - core), rows)
            remote(block, block, s.at[k], r.at[k], sib, start=False).wait_recv()

    with jax.named_scope("spread"):
        for k in sorted(range(1, ny), key=lambda k: -min(k, ny - k)):
            to = yat(k)
            remote(
                st_h.at[:, pl.ds(pl.multiple_of(to * piece, 16), piece), :],
                a2a.at[y], a2a_s.at[k - 1], a2a_r.at[k - 1], ydev(k),
            )
        for ring, _, _ in weights:
            ring.start(1, hz)
        pass_on(0)

    def weight_step(step):
        for ring, _, _ in weights:
            ring.wait(step, hz)
            if step < hz:
                ring.start(step + 1, hz)
        pass_on(step)
        if step < hz:
            pass_on(-step)

    with jax.named_scope("weights_1_2"):
        weight_step(1)
        weight_step(2)

    pick_ring = Ring(
        picked, lambda k: picked.at[yat(k)], pairs // 2, pick_s, pick_r, ydev(1), ydev(-1)
    )
    with jax.named_scope("select"):
        for k in range(1, ny):
            block = a2a.at[yat(-k)]
            remote(block, block, a2a_s.at[k - 1], a2a_r.at[k - 1], ydev(k), start=False).wait_recv()
        local[0].wait()
        names = [owner[i // owner.shape[1], i % owner.shape[1]] for i in range(used)]
        for i in range(used):
            rank = sum([(names[i] == names[j]).astype(jnp.int32) for j in range(i)], jnp.int32(0))
            picked[y, i * piece : (i + 1) * piece, :] = a2a[names[i], jnp.minimum(rank, a2a.shape[1] - 1)]
        pick_ring.start(1, hy)

    with jax.named_scope("weights_3"):
        weight_step(3)
    with jax.named_scope("picked_1"):
        pick_ring.wait(1, hy)
        pick_ring.start(2, hy)
    with jax.named_scope("weights_4"):
        weight_step(4)
    with jax.named_scope("unpack"):
        local[1].wait()
        from_sibling(*weights[0], wo)
        from_sibling(*weights[1], wkv)
        for i in range(cores * nz):
            both = wkv[2 * kw_rows * i : 2 * kw_rows * (i + 1), :].astype(F32)
            kvw_f[kw_rows * i : kw_rows * (i + 1), :proj] = both[:kw_rows]
            kvw_f[kw_rows * i : kw_rows * (i + 1), proj:] = both[kw_rows:]
        kvw[...] = kvw_f[...].astype(BF16)

    per_span = pairs // spans

    def project(k):
        place = yat(k)
        made = dot(picked[place], kvw[...]).astype(BF16)
        at = pl.ds(pl.multiple_of(place * per_span, 16), per_span)
        for u in range(spans):
            kv[1 + u, at, :] = made[u * per_span : (u + 1) * per_span]
        remote(kv.at[spans, at], kv.at[0, at], halo_s.at[k % ny], halo_r.at[k % ny], xdev(1))

    with jax.named_scope("grad_partial"):
        local[3].wait()

        def partial(k):
            rows = rows_of(wo, yat(k), proj)
            gpart[k % ny] = dot(cot[...], rows[...], NT).astype(BF16)

        for k in range(ny):
            partial(hy - k)

    def rs_start(step):
        for way, to in ((0, ydev(1)), (1, ydev(-1))):
            src, dst = rs_out.at[way, step - 1], rs_in.at[way, step - 1]
            if step == 1:
                half = pl.ds(way * (tok // 2), tok // 2)
                src, dst = gpart.at[hy, half], rs_in.at[way, 0, half]
            remote(src, dst, rs_s.at[way, step - 1], rs_r.at[way, step - 1], to)

    def rs_wait(step):
        for way in range(2):
            dst = rs_in.at[way, step - 1]
            if step == 1:
                dst = rs_in.at[way, 0, pl.ds(way * (tok // 2), tok // 2)]
            remote(dst, dst, rs_s.at[way, step - 1], rs_r.at[way, step - 1], ydev(1), start=False).wait_recv()

    def rs_step(step):
        rs_wait(step)
        left = hy - step
        for way, k in ((0, left), (1, ny - left)):
            if step == 1:
                lo, hi = way * (tok // 2), (way + 1) * (tok // 2)
                rs_out[way, step, lo:hi] = (
                    rs_in[way, 0, lo:hi].astype(F32) + gpart[k, lo:hi].astype(F32)
                ).astype(BF16)
                lo, hi = (1 - way) * (tok // 2), (2 - way) * (tok // 2)
                rs_out[way, step, lo:hi] = gpart[k, lo:hi]
            else:
                rs_out[way, step] = (
                    rs_in[way, step - 1].astype(F32) + gpart[k].astype(F32)
                ).astype(BF16)
        rs_start(step + 1)

    with jax.named_scope("rs_1"):
        rs_start(1)
        project(0)
        project(1)
        project(-1)
    with jax.named_scope("picked_2"):
        pick_ring.wait(2, hy)
        pick_ring.start(3, hy)
        project(2)
        project(-2)
    with jax.named_scope("queries"):
        local[2].wait()
        local[4].wait()
        from_sibling(*weights[2], wq)
        qpad[pl.ds(1, tok), :] = dot(hid[...], wq[...]).astype(BF16).astype(F32)
    with jax.named_scope("picked_3"):
        pick_ring.wait(3, hy)
        pick_ring.start(4, hy)
        project(3)
        project(-3)
    with jax.named_scope("rs_2"):
        rs_step(1)
    with jax.named_scope("picked_4"):
        pick_ring.wait(4, hy)
        project(4)
    with jax.named_scope("rs_3"):
        rs_step(2)

    def forward(g):
        rows = pl.ds(g * span, span)
        for h in range(heads):
            cols = pl.ds(h * HEAD_DIM, HEAD_DIM)
            q = qpad[rows, cols].astype(BF16)
            scores = dot(q, kv[g, :, cols], NT) * scale
            e = jnp.exp(scores - jnp.max(scores, axis=-1, keepdims=True))
            p = e / jnp.sum(e, axis=-1, keepdims=True)
            probs[g * heads + h] = p
            out = dot(p.astype(BF16), kv[g, :, pl.ds(proj + h * HEAD_DIM, HEAD_DIM)])
            if g == 0:
                out = jnp.where(x == 0, jnp.zeros_like(out), out)
            apad[rows, cols] = out

    with jax.named_scope("forward"):
        for g in range(1, spans + 1):
            forward(g)
    with jax.named_scope("rs_4"):
        rs_step(3)
    with jax.named_scope("halo"):
        for k in range(ny):
            at = pl.ds(pl.multiple_of(yat(k) * per_span, 16), per_span)
            remote(kv.at[0, at], kv.at[0, at], halo_s.at[k], halo_r.at[k], xdev(1), start=False).wait_recv()
        forward(0)
    att_ring = Ring(att, lambda k: att.at[yat(k)], tok // 2, att_s, att_r, ydev(1), ydev(-1))
    with jax.named_scope("att_1"):
        att[y] = apad[pl.ds(1, tok), :].astype(BF16)
        att_ring.start(1, hy)
    with jax.named_scope("rs_last"):
        rs_wait(hy)
        total = gpart[0].astype(F32) + rs_in[0, hy - 1].astype(F32) + rs_in[1, hy - 1].astype(F32)
        gpad[pl.ds(1, tok), :] = total.astype(BF16).astype(F32)

    def backward(g):
        rows = pl.ds(g * span, span)
        for h in range(heads):
            cols = pl.ds(h * HEAD_DIM, HEAD_DIM)
            p = probs[g * heads + h]
            gp = dot(gpad[rows, cols].astype(BF16), kv[g, :, pl.ds(proj + h * HEAD_DIM, HEAD_DIM)], NT)
            gs = (p * (gp - jnp.sum(p * gp, axis=-1, keepdims=True))).astype(BF16)
            out = dot(gs, kv[g, :, cols]) * scale
            if g == 0:
                out = jnp.where(x == 0, jnp.zeros_like(out), out)
            gqpad[rows, cols] = out

    with jax.named_scope("backward"):
        for g in range(spans + 1):
            backward(g)
        gqt[...] = gqpad[pl.ds(1, tok), :].astype(BF16).astype(F32).T.astype(BF16)

    wide = grad_o.shape[0]

    def weight_grad(p, c):
        block = zat(p + 1) * cores + c
        return dot(gqt[...], hid[:, pl.ds(pl.multiple_of(block * wide, 128), wide)])

    with jax.named_scope("to_sibling"):
        for p in range(nz):
            sib_out[p] = weight_grad(p, 1 - core).astype(BF16)
            remote(sib_out.at[p], sib_in.at[p], sib_s.at[p], sib_r.at[p], sib)
    with jax.named_scope("att_2"):
        att_ring.wait(1, hy)
        att_ring.start(2, hy)

    quarter = proj // nx
    batch = nz // 2

    def x_copy(b, k, start):
        to = pl.ds(pl.multiple_of(xat(k) * quarter, 16), quarter)
        return remote(
            xs.at[pl.ds(b * batch, batch), to], x_in.at[k - 1, pl.ds(b * batch, batch)],
            x_s.at[b, k - 1], x_r.at[b, k - 1], xdev(k), start,
        )

    with jax.named_scope("to_x"):
        for p in range(nz):
            mine = weight_grad(p, core).astype(BF16).astype(F32)
            remote(sib_in.at[p], sib_in.at[p], sib_s.at[p], sib_r.at[p], sib, start=False).wait_recv()
            xs[p] = (mine + sib_in[p].astype(F32)).astype(BF16)
            if p % batch == batch - 1:
                for k in range(1, nx):
                    x_copy(p // batch, k, True)

    def mix(k):
        rows = rows_of(wo, yat(k), proj)
        made = dot(att[yat(k)], rows[...])
        if k == 0:
            acc[...] = made
        else:
            acc[...] += made

    with jax.named_scope("att_3"):
        att_ring.wait(2, hy)
        att_ring.start(3, hy)
        mix(0)
        mix(1)
        mix(-1)

    own_quarter = pl.ds(pl.multiple_of(x * quarter, 16), quarter)

    def z_send(b):
        for k in range(1, nx):
            x_copy(b, k, False).wait_recv()
        for p in range(b * batch, (b + 1) * batch):
            total = xs[p, own_quarter, :].astype(F32)
            for k in range(1, nx):
                total += x_in[k - 1, p].astype(F32)
            zs[p] = total.astype(BF16)
            if p + 1 < nz:
                remote(zs.at[p], z_in.at[p], z_s.at[p], z_r.at[p], zdev(p + 1))

    with jax.named_scope("to_z"):
        z_send(0)
    with jax.named_scope("att_4"):
        att_ring.wait(3, hy)
        att_ring.start(4, hy)
        mix(2)
        mix(-2)
    with jax.named_scope("to_z_2"):
        z_send(1)
        mix(3)
        mix(-3)
    with jax.named_scope("from_z"):
        total = zs[nz - 1].astype(F32)
        for p in range(nz - 1):
            remote(zs.at[p], z_in.at[p], z_s.at[p], z_r.at[p], zdev(p + 1), start=False).wait_recv()
            total += z_in[p].astype(F32)
        fin[x] = total.astype(BF16)
        for k in range(1, nx):
            remote(fin.at[x], fin.at[x], f_s.at[k - 1], f_r.at[k - 1], xdev(k))
    with jax.named_scope("mixed"):
        att_ring.wait(4, hy)
        mix(4)
        mixed_o[...] = acc[...].astype(BF16)
    with jax.named_scope("from_x"):
        for k in range(1, nx):
            block = fin.at[xat(-k)]
            remote(block, block, f_s.at[k - 1], f_r.at[k - 1], xdev(k), start=False).wait_recv()
        grad_o[...] = fin[...].astype(F32).reshape(proj, wide).T
    with jax.named_scope("drain"):
        for copy in sent + wo_ring.sent + wq_ring.sent + kw_ring.sent + pick_ring.sent + att_ring.sent:
            copy.wait_send()


def shards(sizes, hidden, states, owner, query_w, key_w, value_w, out_w, cotangent):
    cores, nz, nx, ny = sizes
    tok, wide = hidden.shape
    slots, length, enc_d = states.shape
    spans, per = owner.shape
    proj = query_w.shape[1]
    heads = proj // HEAD_DIM
    n_dp = cores * nz
    used = spans * per
    piece = length // ny
    pairs = used * piece
    cols = out_w.shape[1]
    keys = per * length
    padded = tok + tok // spans
    dma = pltpu.SemaphoreType.DMA
    any_, vmem = pl.BlockSpec(memory_space=pl.ANY), pl.BlockSpec(memory_space=pltpu.VMEM)
    quarter = proj // nx
    scratch = [
        pltpu.VMEM((tok, wide), BF16),
        pltpu.VMEM((tok, cols), BF16),
        pltpu.VMEM((wide, proj), BF16),
        pltpu.VMEM((n_dp * out_w.shape[0], cols), BF16),
        pltpu.VMEM((2 * enc_d, proj), BF16),
        pltpu.VMEM((enc_d, 2 * proj), F32),
        pltpu.VMEM((enc_d, 2 * proj), BF16),
        pltpu.VMEM((ny, slots, piece, enc_d), BF16),
        pltpu.VMEM((ny, pairs, enc_d), BF16),
        pltpu.VMEM((spans + 1, keys, 2 * proj), BF16),
        pltpu.VMEM((ny, tok, proj), BF16),
        pltpu.VMEM((2, ny // 2, tok, proj), BF16),
        pltpu.VMEM((2, ny // 2, tok, proj), BF16),
        pltpu.VMEM((padded, proj), F32),
        pltpu.VMEM((padded, proj), F32),
        pltpu.VMEM(((spans + 1) * heads, tok // spans, keys), F32),
        pltpu.VMEM((padded, proj), F32),
        pltpu.VMEM((ny, tok, proj), BF16),
        pltpu.VMEM((padded, proj), F32),
        pltpu.VMEM((proj, tok), BF16),
        pltpu.VMEM((nz, proj, wide // n_dp), BF16),
        pltpu.VMEM((nz, proj, wide // n_dp), BF16),
        pltpu.VMEM((nz, proj, wide // n_dp), BF16),
        pltpu.VMEM((nx - 1, nz, quarter, wide // n_dp), BF16),
        pltpu.VMEM((nz, quarter, wide // n_dp), BF16),
        pltpu.VMEM((nz - 1, quarter, wide // n_dp), BF16),
        pltpu.VMEM((nx, quarter, wide // n_dp), BF16),
        pltpu.VMEM((tok, cols), F32),
        dma((5,)),
        dma((ny - 1,)), dma((ny - 1,)),
        dma((2, ny // 2)), dma((2, ny // 2)),
        dma((2, ny // 2)), dma((2, ny // 2)),
        dma((2, ny // 2)), dma((2, ny // 2)),
        dma((2, nz // 2)), dma((2, nz // 2)),
        dma((2, nz // 2)), dma((2, nz // 2)),
        dma((2, nz // 2)), dma((2, nz // 2)),
        dma((nz,)), dma((nz,)), dma((nz,)), dma((nz,)), dma((nz,)), dma((nz,)),
        dma((ny,)), dma((ny,)),
        dma((nz,)), dma((nz,)),
        dma((2, nx - 1)), dma((2, nx - 1)),
        dma((nz - 1,)), dma((nz - 1,)),
        dma((nx - 1,)), dma((nx - 1,)),
    ]
    return pl.pallas_call(
        functools.partial(kernel, cores, nz, nx, ny, spans),
        out_shape=(
            jax.ShapeDtypeStruct((tok, cols), BF16),
            jax.ShapeDtypeStruct((wide // n_dp, proj), F32),
        ),
        in_specs=[any_, any_, pl.BlockSpec(memory_space=pltpu.SMEM), any_, vmem, vmem, any_, any_],
        out_specs=(vmem, vmem),
        scratch_shapes=scratch,
        compiler_params=pltpu.CompilerParams(
            collective_id=0, has_side_effects=True, vmem_limit_bytes=48 * 2**20
        ),
        cost_estimate=pl.CostEstimate(flops=3 * 10**9, bytes_accessed=8 * 2**20, transcendentals=163840),
    )(hidden, states, owner, query_w, key_w, value_w, out_w, cotangent)


def solution(mesh):
    sizes = (2, mesh.shape["dp"] // 2, mesh.shape["ctx"], mesh.shape["enc"])
    in_specs = (
        P(("dp", "ctx"), None),
        P(("dp", "ctx", "enc"), None, None),
        P(("dp", "ctx"), None),
        P("dp", "enc"),
        P("dp", "enc"),
        P("dp", "enc"),
        P("dp", "enc"),
        P(("dp", "ctx"), "enc"),
    )
    out_specs = (P(("dp", "ctx"), "enc"), P("dp", "enc"))
    return jax.shard_map(
        functools.partial(shards, sizes),
        mesh=mesh,
        in_specs=in_specs,
        out_specs=out_specs,
        check_vma=False,
    )
```

time: 290 us -> 111 us (0.38)
  the two profiles are of different devices: /device:TPU:24 before, /device:TPU:16 now
where the time goes in v1:
time: 111 us; the launch traced here: 110 us
  Pallas kernels  100 us (90%)
  local copies, waits for them, and re-layouts  9.11 us (8%)
    pallas_call x1, Pallas kernels, shards(): pl.pallas_call(functools.partial(kernel, cores, nz, nx, ny, spans), out_s...  100 us
    unnamed x17, local copies, waits for them, and re-layouts  9.11 us

profile of v1, /device:TPU:16, one launch (start us, length us, event | category | flops | bytes accessed | tf_op | source)
XLA Modules:
  0.0 110.2 jit_solution(10062317286977879443)
XLA Ops:
  0.6 0.8 copy.10.owner
  1.4 0.0 copy-start
  1.4 1.6 %copy-done = bf16[256,4096]{1,0:T(8,128)(2,1)S(1)} copy-done((bf16[256,4096]{1,0:T(8,128)(2,1)S(1)}, bf16[256,4096]{1,0:T(8,128)(2,1)}, u32[]{:S(2)}) %copy-start) | copy-done | bytes 2097176
  3.0 0.0 copy-start.1
  3.0 1.1 copy-done.1
  4.1 0.0 copy-start.2
  4.1 0.9 copy-done.2
  5.0 0.0 copy-start.3
  5.0 0.9 copy-done.3
  5.9 0.0 copy-start.4
  5.9 0.9 copy-done.4
  6.8 0.0 copy-start.5
  6.8 0.7 copy-done.5
  7.6 0.0 copy-start.6
  7.6 0.7 copy-done.6
  8.3 100.4 %shard_map.95 = (bf16[256,512]{1,0:T(8,128)(2,1)S(1)}, f32[256,256]{1,0:T(8,128)S(1)}) custom-call(bf16[256,4096]{1,0:T(8,128)(2,1)S(1)} %copy-done, bf16[3,128,896]{2,1,0:T(8,128)(2,1)S(1)} %copy-done.1, s32[4,2]{1,0:T(4,128)S(1)} %copy.10.owner, bf16[256,256]{1,0:T(8,128)(2,1)S(1)} %copy-done.3, bf16[56,256]{1,0:T(8,128)(2,1)S(1)} %copy-done.5, ...), custom_call_target="tpu_custom_call" | custom-call | flops 3000000000 | bytes 8388608 | tf_op jit(solution)/shard_map/pallas_call | solution.py:508
  108.8 0.7 copy.13
  109.5 0.7 copy.14
Async XLA Ops:
  1.4 1.6 %copy-start = (bf16[256,4096]{1,0:T(8,128)(2,1)S(1)}, bf16[256,4096]{1,0:T(8,128)(2,1)}, u32[]{:S(2)}) copy-start(bf16[256,4096]{1,0:T(8,128)(2,1)} %hid_h.1) | copy-start | bytes 6291460
  3.0 1.1 copy-start.1
  4.1 0.9 copy-start.2
  5.0 0.9 copy-start.3
  5.9 0.9 copy-start.4
  6.8 0.7 copy-start.5
  7.6 0.7 copy-start.6

commit v2 on v1

v2 whole, which is shorter than its diff:
```python
import functools
import math

import jax
import jax.numpy as jnp
from jax import lax
from jax.experimental import pallas as pl
from jax.experimental.pallas import tpu as pltpu
from jax.sharding import PartitionSpec as P

HEAD_DIM = 128
MESH = pl.DeviceIdType.MESH
BF16 = jnp.bfloat16
F32 = jnp.float32
NT = (((1,), (1,)), ((), ()))


def dot(a, b, dims=(((1,), (0,)), ((), ()))):
    return lax.dot_general(a, b, dims, preferred_element_type=F32)


def rows_of(ref, index, count):
    step = 128 if count % 128 == 0 else 16
    return ref.at[pl.ds(pl.multiple_of(index * count, step), count)]


class Ring:
    def __init__(self, slot, first, send, recv, right, left, own=None, number=0):
        self.slot, self.number = slot, number
        self.first, self.send, self.recv = first, send, recv
        self.right, self.left, self.own = right, left, own
        self.sent = []

    def part(self, ref, half):
        if half == 0:
            return ref.at[pl.ds(0, self.first)]
        return ref.at[pl.ds(self.first, ref.shape[0] - self.first)]

    def start(self, step, last):
        for way, to, sign in ((0, self.right, -1), (1, self.left, 1)):
            dst = self.slot(sign * (step - 1))
            src = self.own if step == 1 and self.own is not None else dst
            if step == last:
                src, dst = self.part(src, way), self.part(dst, way)
            copy = pltpu.make_async_remote_copy(
                src_ref=src,
                dst_ref=dst,
                send_sem=self.send.at[way, step - 1],
                recv_sem=self.recv.at[way, step - 1],
                device_id=to,
                device_id_type=MESH,
            )
            copy.start()
            self.sent.append(copy)

    def wait(self, step, last):
        for way, sign in ((0, -1), (1, 1)):
            dst = self.slot(sign * step)
            if step == last:
                dst = self.part(dst, way)
            pltpu.make_async_remote_copy(
                src_ref=dst,
                dst_ref=dst,
                send_sem=self.send.at[way, step - 1],
                recv_sem=self.recv.at[way, step - 1],
                device_id=self.right,
                device_id_type=MESH,
            ).wait_recv()


def kernel(
    cores, nz, nx, ny, spans, hid_h, st_h, owner, wq_h, wk_h, wv_h, wo_h, cot_h, mixed_o, grad_o,
    hid, cot, wk_v, wv_v, wq, wo, wkv, kvw_f, kvw, a2a, picked, kv, gpart, rs_out, rs_in, qpad, gpad, probs,
    apad, att, gqpad, ht, hx, gq, part, sib_out, sib_in, zs, z_in, fin, acc,
    local_sem, a2a_s, a2a_r, pick_s, pick_r, rs_s, rs_r, att_s, att_r,
    wo_s, wo_r, wq_s, wq_r, kw_s, kw_r, wo_cs, wo_cr, wq_cs, wq_cr, kw_cs, kw_cr, wq_xs, wq_xr,
    halo_s, halo_r, hx_s, hx_r, gq_s, gq_r, sib_s, sib_r, z_s, z_r, f_s, f_r,
):
    dp, x, y = lax.axis_index("dp"), lax.axis_index("ctx"), lax.axis_index("enc")
    z, core = lax.div(dp, cores), lax.rem(dp, cores)
    sib = {"dp": z * cores + (1 - core)}

    def zat(k):
        return lax.rem(z + (k + nz), nz)

    def xat(k):
        return lax.rem(x + (k + nx), nx)

    def yat(k):
        return lax.rem(y + (k + ny), ny)

    def zdev(k):
        return {"dp": zat(k) * cores + core}

    def xdev(k):
        return {"ctx": xat(k)}

    def ydev(k):
        return {"enc": yat(k)}

    hy, hz = ny // 2, nz // 2
    tok = hid.shape[0]
    proj = wq_h.shape[1]
    wide = wq_h.shape[0]
    quarter = wide // nx
    heads = proj // HEAD_DIM
    span = tok // spans
    pairs = picked.shape[1]
    used = owner.shape[0] * owner.shape[1]
    piece = pairs // used
    kw_rows = wk_v.shape[0]
    scale = 1.0 / math.sqrt(HEAD_DIM)
    sent = []

    def remote(src, dst, s, r, to, start=True):
        copy = pltpu.make_async_remote_copy(
            src_ref=src, dst_ref=dst, send_sem=s, recv_sem=r, device_id=to, device_id_type=MESH
        )
        if start:
            copy.start()
            sent.append(copy)
        return copy

    with jax.named_scope("entry"):
        barrier = pltpu.get_barrier_semaphore()
        peers = [sib]
        peers += [ydev(k) for k in range(1, ny)]
        peers += [xdev(k) for k in range(1, nx)]
        peers += [zdev(k) for k in range(1, nz)]
        for peer in peers:
            pl.semaphore_signal(barrier, inc=1, device_id=peer, device_id_type=MESH)

        local = [
            pltpu.make_async_copy(st_h.at[:, pl.ds(pl.multiple_of(y * piece, 16), piece), :], a2a.at[y], local_sem.at[0]),
            pltpu.make_async_copy(wo_h, rows_of(wo, dp, wo_h.shape[0]), local_sem.at[1]),
            pltpu.make_async_copy(wq_h, wq.at[z, core], local_sem.at[2]),
            pltpu.make_async_copy(cot_h, cot, local_sem.at[3]),
            pltpu.make_async_copy(hid_h, hid, local_sem.at[4]),
            pltpu.make_async_copy(wk_h, wk_v, local_sem.at[5]),
            pltpu.make_async_copy(wv_h, wv_v, local_sem.at[6]),
        ]
        for copy in local:
            copy.start()
        local[5].wait()
        local[6].wait()
        rows_of(wkv, dp, 2 * kw_rows)[...] = jnp.concatenate(
            [wk_v[...].astype(F32), wv_v[...].astype(F32)], axis=0
        ).astype(BF16)
        qpad[...] = jnp.zeros_like(qpad)
        gpad[...] = jnp.zeros_like(gpad)
        pl.semaphore_wait(barrier, len(peers))

    class Weight:
        def __init__(self, buf, own, cuts, s, r, to_sib, from_sib):
            self.rows = buf.shape[0] // (cores * nz)
            self.buf, self.own, self.s, self.r = buf, own, to_sib, from_sib
            self.rings = []
            for n, (lo, hi) in enumerate(zip(cuts, [*cuts[1:], self.rows])):
                part = pl.ds(lo, hi - lo)
                self.rings.append(
                    Ring(
                        lambda k, part=part: self.block(k, core).at[part],
                        (hi - lo + 16) // 32 * 16, s.at[n], r.at[n], zdev(1), zdev(-1),
                        None if own is None else own.at[part],
                    )
                )

        def block(self, k, c):
            return rows_of(self.buf, zat(k) * cores + c, self.rows)

        def start(self):
            for ring in self.rings:
                ring.start(1, hz)
            self.pass_on(0)

        def pass_on(self, k):
            block = self.block(k, core)
            src = self.own if k == 0 and self.own is not None else block
            remote(src, block, self.s.at[k % nz], self.r.at[k % nz], sib)

        def wait(self, step):
            for ring in self.rings:
                ring.wait(step, hz)
                if step < hz:
                    ring.start(step + 1, hz)
            self.pass_on(step)
            if step < hz:
                self.pass_on(-step)

        def from_sibling(self):
            for k in range(nz):
                block = self.block(k, 1 - core)
                remote(block, block, self.s.at[k], self.r.at[k], sib, start=False).wait_recv()

    out_w = Weight(wo, wo_h, (0, wo_h.shape[0] // 2), wo_s, wo_r, wo_cs, wo_cr)
    kv_w = Weight(wkv, None, (0,), kw_s, kw_r, kw_cs, kw_cr)

    def query_piece(k, q):
        return wq.at[zat(k), core, pl.ds(pl.multiple_of(q * quarter, 16), quarter)]

    own_piece = wq_h.at[pl.ds(pl.multiple_of(x * quarter, 16), quarter)]
    query_ring = Ring(lambda k: query_piece(k, x), quarter // 2, wq_s, wq_r, zdev(1), zdev(-1), own_piece)

    def query_pass(k):
        dst = query_piece(k, x)
        for j in range(1, nx):
            remote(dst, dst, wq_xs.at[k % nz - 1, j - 1], wq_xr.at[k % nz - 1, j - 1], xdev(j))

    def query_wait(step):
        query_ring.wait(step, hz)
        if step < hz:
            query_ring.start(step + 1, hz)
        query_pass(step)
        if step < hz:
            query_pass(-step)

    def query_all():
        for k in range(1, nz):
            for j in range(1, nx):
                block = query_piece(k, xat(-j))
                remote(block, block, wq_xs.at[k - 1, j - 1], wq_xr.at[k - 1, j - 1], xdev(j), start=False).wait_recv()
        local[2].wait()
        remote(wq.at[:, core], wq.at[:, core], wq_cs, wq_cr, sib)

    def query_from_sibling():
        block = wq.at[:, 1 - core]
        remote(block, block, wq_cs, wq_cr, sib, start=False).wait_recv()

    with jax.named_scope("spread"):
        for k in sorted(range(1, ny), key=lambda k: -min(k, ny - k)):
            to = yat(k)
            remote(
                st_h.at[:, pl.ds(pl.multiple_of(to * piece, 16), piece), :],
                a2a.at[y], a2a_s.at[k - 1], a2a_r.at[k - 1], ydev(k),
            )
    with jax.named_scope("weights_0"):
        out_w.start()
        kv_w.start()
        query_ring.start(1, hz)
    with jax.named_scope("hidden_x"):
        local[4].wait()
        for b in range(cores * nz):
            ht[b // cores, b % cores] = hid[:, b * wide : (b + 1) * wide].T
        for j in range(1, nx):
            part_x = pl.ds(pl.multiple_of(xat(j) * quarter, 16), quarter)
            remote(ht.at[:, :, part_x], hx.at[x], hx_s.at[j - 1], hx_r.at[j - 1], xdev(j))
    with jax.named_scope("weights_1"):
        for step in (1, 2):
            out_w.wait(step)
            kv_w.wait(step)
            query_wait(step)

    chunks = 2
    share = tok // chunks

    def rs_move(chunk, way, step):
        lo, rows = chunk * share, share
        src = rs_out.at[way, step - 1, pl.ds(lo, rows)]
        if step == 1:
            rows = share // 2
            lo += way * rows
            src = gpart.at[hy, pl.ds(lo, rows)]
        dst = rs_in.at[way, step - 1, pl.ds(lo, rows)]
        return src, dst, rs_s.at[chunk, way, step - 1], rs_r.at[chunk, way, step - 1]

    def rs_start(chunk, step):
        for way, to in ((0, ydev(1)), (1, ydev(-1))):
            remote(*rs_move(chunk, way, step), to)

    def rs_wait(chunk, step):
        for way in range(2):
            _, dst, s, r = rs_move(chunk, way, step)
            remote(dst, dst, s, r, ydev(1), start=False).wait_recv()

    def rs_step(step):
        left = hy - step
        for chunk in range(chunks):
            rs_wait(chunk, step)
            for way, k in ((0, left), (1, ny - left)):
                lo, hi = chunk * share, (chunk + 1) * share
                if step == 1:
                    half = share // 2
                    other = lo + (1 - way) * half
                    rs_out[way, step, other : other + half] = gpart[k, other : other + half]
                    lo += way * half
                    hi = lo + half
                rs_out[way, step, lo:hi] = (
                    rs_in[way, step - 1, lo:hi].astype(F32) + gpart[k, lo:hi].astype(F32)
                ).astype(BF16)
            rs_start(chunk, step + 1)

    part_rows = pairs // chunks

    def pick_slot(chunk):
        return lambda k: picked.at[yat(k), pl.ds(chunk * part_rows, part_rows)]

    order = tuple(reversed(range(chunks)))
    pick_rings = {
        c: Ring(pick_slot(c), part_rows // 2, pick_s.at[c], pick_r.at[c], ydev(1), ydev(-1)) for c in order
    }

    def pick_start(step):
        for c in order:
            pick_rings[c].start(step, hy)

    def pick_wait(step):
        for c in order:
            pick_rings[c].wait(step, hy)
            if step < hy:
                pick_rings[c].start(step + 1, hy)

    with jax.named_scope("select"):
        for k in range(1, ny):
            block = a2a.at[yat(-k)]
            remote(block, block, a2a_s.at[k - 1], a2a_r.at[k - 1], ydev(k), start=False).wait_recv()
        local[0].wait()
        names = [owner[i % owner.shape[0], i // owner.shape[0]] for i in range(used)]
        for i in range(used):
            rank = sum([(names[i] == names[j]).astype(jnp.int32) for j in range(i)], jnp.int32(0))
            rank = jnp.minimum(rank, a2a.shape[1] - 1)
            picked[y, i * piece : (i + 1) * piece, :] = a2a[names[i], rank]
    with jax.named_scope("picked_0"):
        pick_start(1)
    with jax.named_scope("weights_2"):
        out_w.wait(3)
        out_w.wait(4)
        local[1].wait()
        out_w.from_sibling()
    with jax.named_scope("grad_partial"):
        local[3].wait()
        for k in range(ny):
            rows = rows_of(wo, yat(hy - k), proj)
            gpart[(hy - k) % ny] = dot(cot[...], rows[...], NT).astype(BF16)
    with jax.named_scope("rs_1"):
        for chunk in range(chunks):
            rs_start(chunk, 1)
    with jax.named_scope("picked_1"):
        pick_wait(1)
    with jax.named_scope("weights_3"):
        kv_w.wait(3)
        query_wait(3)
        kv_w.wait(4)
        query_wait(4)
        kv_w.from_sibling()
    with jax.named_scope("unpack"):
        for i in range(cores * nz):
            both = wkv[2 * kw_rows * i : 2 * kw_rows * (i + 1), :].astype(F32)
            kvw_f[kw_rows * i : kw_rows * (i + 1), :proj] = both[:kw_rows]
            kvw_f[kw_rows * i : kw_rows * (i + 1), proj:] = both[kw_rows:]
        kvw[...] = kvw_f[...].astype(BF16)

    per_span = pairs // spans

    def project(ks):
        for chunk in order:
            rows = slice(chunk * part_rows, (chunk + 1) * part_rows)
            made = dot(jnp.concatenate([picked[yat(k), rows, :] for k in ks], axis=0), kvw[...]).astype(BF16)
            for n, k in enumerate(ks):
                at = pl.ds(pl.multiple_of(yat(k) * per_span, 16), per_span)
                for u in range(spans // chunks):
                    lo = n * part_rows + u * per_span
                    kv[1 + chunk * (spans // chunks) + u, at, :] = made[lo : lo + per_span]
                if chunk == chunks - 1:
                    remote(kv.at[spans, at], kv.at[0, at], halo_s.at[k % ny], halo_r.at[k % ny], xdev(1))

    with jax.named_scope("project_1"):
        project((0, 1))
    with jax.named_scope("picked_2"):
        pick_wait(2)
    with jax.named_scope("rs_2"):
        rs_step(1)
    with jax.named_scope("project_2"):
        project((-1, 2))
    with jax.named_scope("picked_3"):
        pick_wait(3)
    with jax.named_scope("rs_3"):
        rs_step(2)
    with jax.named_scope("weights_5"):
        query_all()
        query_from_sibling()
    with jax.named_scope("queries"):
        qpad[pl.ds(1, tok), :] = dot(hid[...], wq[...].reshape(hid.shape[1], proj)).astype(BF16).astype(F32)
    with jax.named_scope("project_3"):
        project((-2, 3, -3))
    with jax.named_scope("picked_4"):
        pick_wait(4)
        project((4,))
    with jax.named_scope("rs_4"):
        rs_step(3)

    def forward(g):
        rows = pl.ds(g * span, span)
        for h in range(heads):
            cols = pl.ds(h * HEAD_DIM, HEAD_DIM)
            q = qpad[rows, cols].astype(BF16)
            scores = dot(q, kv[g, :, cols], NT) * scale
            e = jnp.exp(scores - jnp.max(scores, axis=-1, keepdims=True))
            p = e / jnp.sum(e, axis=-1, keepdims=True)
            probs[g * heads + h] = p
            out = dot(p.astype(BF16), kv[g, :, pl.ds(proj + h * HEAD_DIM, HEAD_DIM)])
            if g == 0:
                out = jnp.where(x == 0, jnp.zeros_like(out), out)
            apad[rows, cols] = out

    with jax.named_scope("forward"):
        for g in range(1, spans + 1):
            forward(g)
    with jax.named_scope("halo"):
        for k in range(ny):
            at = pl.ds(pl.multiple_of(yat(k) * per_span, 16), per_span)
            remote(kv.at[0, at], kv.at[0, at], halo_s.at[k], halo_r.at[k], xdev(1), start=False).wait_recv()
        forward(0)

    def att_slot(chunk):
        return lambda k: att.at[yat(k), pl.ds(chunk * share, share)]

    att_rings = [
        Ring(att_slot(c), share // 2, att_s.at[c], att_r.at[c], ydev(1), ydev(-1)) for c in range(chunks)
    ]

    def att_wait(step):
        for ring in att_rings:
            ring.wait(step, hy)
            if step < hy:
                ring.start(step + 1, hy)

    with jax.named_scope("att_1"):
        att[y] = apad[pl.ds(1, tok), :].astype(BF16)
        for ring in att_rings:
            ring.start(1, hy)
    with jax.named_scope("rs_last"):
        for chunk in range(chunks):
            rs_wait(chunk, hy)
        total = gpart[0].astype(F32) + rs_in[0, hy - 1].astype(F32) + rs_in[1, hy - 1].astype(F32)
        gpad[pl.ds(1, tok), :] = total.astype(BF16).astype(F32)

    def backward(g, h):
        rows = pl.ds(g * span, span)
        cols = pl.ds(h * HEAD_DIM, HEAD_DIM)
        p = probs[g * heads + h]
        gp = dot(gpad[rows, cols].astype(BF16), kv[g, :, pl.ds(proj + h * HEAD_DIM, HEAD_DIM)], NT)
        gs = (p * (gp - jnp.sum(p * gp, axis=-1, keepdims=True))).astype(BF16)
        out = dot(gs, kv[g, :, cols]) * scale
        if g == 0:
            out = jnp.where(x == 0, jnp.zeros_like(out), out)
        gqpad[rows, cols] = out

    def mix(k):
        rows = rows_of(wo, yat(k), proj)
        made = dot(att[yat(k)], rows[...])
        if k == 0:
            acc[...] = made
        else:
            acc[...] += made

    def gq_copy(h, j, start):
        block = gq.at[h, x] if start else gq.at[h, xat(-j)]
        return remote(block, block, gq_s.at[h, j - 1], gq_r.at[h, j - 1], xdev(j), start)

    with jax.named_scope("backward"):
        for h in range(heads):
            for g in range(spans + 1):
                backward(g, h)
            gq[h, x] = gqpad[pl.ds(1, tok), pl.ds(h * HEAD_DIM, HEAD_DIM)].astype(BF16)
            for j in range(1, nx):
                gq_copy(h, j, True)

    many = nz * cores * quarter

    with jax.named_scope("own_part"):
        mine = ht[:, :, pl.ds(pl.multiple_of(x * quarter, 16), quarter), :].reshape(many, tok)
        for h in range(heads):
            part[h] = dot(mine, gq[h, x]).reshape(nz, cores, quarter, HEAD_DIM)
        for j in range(1, nx):
            block = hx.at[xat(-j)]
            remote(block, block, hx_s.at[j - 1], hx_r.at[j - 1], xdev(j), start=False).wait_recv()

    def sib_copy(h, start):
        return remote(sib_out.at[h], sib_in.at[h], sib_s.at[h], sib_r.at[h], sib, start)

    def other_parts(h):
        for j in (1, nx - 1, *range(2, nx - 1)):
            gq_copy(h, j, False).wait_recv()
            place = xat(-j)
            part[h] += dot(hx[place].reshape(many, tok), gq[h, place]).reshape(nz, cores, quarter, HEAD_DIM)
        sib_out[h] = part[h, :, 1 - core].astype(BF16)
        sib_copy(h, True)

    def z_copy(h, p, start):
        return remote(zs.at[h, p], z_in.at[h, p], z_s.at[h, p], z_r.at[h, p], zdev(p + 1), start)

    def to_z(h):
        sib_copy(h, False).wait_recv()
        for p in range(nz):
            zs[h, p] = (part[h, zat(p + 1), core] + sib_in[h, zat(p + 1)].astype(F32)).astype(BF16)
            if p + 1 < nz:
                z_copy(h, p, True)

    def f_copy(h, j, start):
        block = fin.at[h, x] if start else fin.at[h, xat(-j)]
        return remote(block, block, f_s.at[h, j - 1], f_r.at[h, j - 1], xdev(j), start)

    def from_z(h):
        total = zs[h, nz - 1].astype(F32)
        for p in range(nz - 1):
            z_copy(h, p, False).wait_recv()
            total += z_in[h, p].astype(F32)
        fin[h, x] = total.astype(BF16)
        for j in range(1, nx):
            f_copy(h, j, True)

    with jax.named_scope("att_2"):
        att_wait(1)
    with jax.named_scope("part_0"):
        other_parts(0)
    with jax.named_scope("att_3"):
        att_wait(2)
    with jax.named_scope("to_z_0"):
        to_z(0)
    with jax.named_scope("part_1"):
        other_parts(1)
    with jax.named_scope("att_4"):
        att_wait(3)
    with jax.named_scope("to_z_1"):
        to_z(1)
    with jax.named_scope("mixed"):
        for k in (0, 1, -1, 2, -2, 3, -3):
            mix(k)
        att_wait(4)
        mix(4)
        mixed_o[...] = acc[...].astype(BF16)
    with jax.named_scope("from_z"):
        for h in range(heads):
            from_z(h)
    with jax.named_scope("from_x"):
        for h in range(heads):
            for j in range(1, nx):
                f_copy(h, j, False).wait_recv()
            grad_o[:, pl.ds(h * HEAD_DIM, HEAD_DIM)] = fin[h].astype(F32).reshape(wide, HEAD_DIM)
    with jax.named_scope("drain"):
        for copy in sent + [
            c for ring in (*out_w.rings, *kv_w.rings, query_ring, *pick_rings.values(), *att_rings) for c in ring.sent
        ]:
            copy.wait_send()


def shards(sizes, hidden, states, owner, query_w, key_w, value_w, out_w, cotangent):
    cores, nz, nx, ny = sizes
    tok, wide = hidden.shape
    slots, length, enc_d = states.shape
    spans, per = owner.shape
    proj = query_w.shape[1]
    heads = proj // HEAD_DIM
    n_dp = cores * nz
    used = spans * per
    piece = length // ny
    pairs = used * piece
    cols = out_w.shape[1]
    keys = per * length
    padded = tok + tok // spans
    dma = pltpu.SemaphoreType.DMA
    any_, vmem = pl.BlockSpec(memory_space=pltpu.HBM), pl.BlockSpec(memory_space=pltpu.VMEM)
    block = wide // n_dp
    quarter = block // nx
    scratch = [
        pltpu.VMEM((tok, wide), BF16),
        pltpu.VMEM((tok, cols), BF16),
        pltpu.VMEM(key_w.shape, BF16),
        pltpu.VMEM(key_w.shape, BF16),
        pltpu.VMEM((nz, cores, block, proj), BF16),
        pltpu.VMEM((n_dp * out_w.shape[0], cols), BF16),
        pltpu.VMEM((2 * enc_d, proj), BF16),
        pltpu.VMEM((enc_d, 2 * proj), F32),
        pltpu.VMEM((enc_d, 2 * proj), BF16),
        pltpu.VMEM((ny, slots, piece, enc_d), BF16),
        pltpu.VMEM((ny, pairs, enc_d), BF16),
        pltpu.VMEM((spans + 1, keys, 2 * proj), BF16),
        pltpu.VMEM((ny, tok, proj), BF16),
        pltpu.VMEM((2, ny // 2, tok, proj), BF16),
        pltpu.VMEM((2, ny // 2, tok, proj), BF16),
        pltpu.VMEM((padded, proj), F32),
        pltpu.VMEM((padded, proj), F32),
        pltpu.VMEM(((spans + 1) * heads, tok // spans, keys), F32),
        pltpu.VMEM((padded, proj), F32),
        pltpu.VMEM((ny, tok, proj), BF16),
        pltpu.VMEM((padded, proj), F32),
        pltpu.VMEM((nz, cores, block, tok), BF16),
        pltpu.VMEM((nx, nz, cores, quarter, tok), BF16),
        pltpu.VMEM((heads, nx, tok, HEAD_DIM), BF16),
        pltpu.VMEM((heads, nz, cores, quarter, HEAD_DIM), F32),
        pltpu.VMEM((heads, nz, quarter, HEAD_DIM), BF16),
        pltpu.VMEM((heads, nz, quarter, HEAD_DIM), BF16),
        pltpu.VMEM((heads, nz, quarter, HEAD_DIM), BF16),
        pltpu.VMEM((heads, nz - 1, quarter, HEAD_DIM), BF16),
        pltpu.VMEM((heads, nx, quarter, HEAD_DIM), BF16),
        pltpu.VMEM((tok, cols), F32),
        dma((7,)),
        dma((ny - 1,)), dma((ny - 1,)),
        dma((2, 2, ny // 2)), dma((2, 2, ny // 2)),
        dma((2, 2, ny // 2)), dma((2, 2, ny // 2)),
        dma((2, 2, ny // 2)), dma((2, 2, ny // 2)),
        dma((2, 2, nz // 2)), dma((2, 2, nz // 2)),
        dma((2, nz // 2)), dma((2, nz // 2)),
        dma((1, 2, nz // 2)), dma((1, 2, nz // 2)),
        dma((nz,)), dma((nz,)), dma(()), dma(()), dma((nz,)), dma((nz,)),
        dma((nz - 1, nx - 1)), dma((nz - 1, nx - 1)),
        dma((ny,)), dma((ny,)),
        dma((nx - 1,)), dma((nx - 1,)),
        dma((heads, nx - 1)), dma((heads, nx - 1)),
        dma((heads,)), dma((heads,)),
        dma((heads, nz - 1)), dma((heads, nz - 1)),
        dma((heads, nx - 1)), dma((heads, nx - 1)),
    ]
    operands = [
        pltpu.with_memory_space_constraint(a, pltpu.HBM)
        for a in (hidden, states, query_w, key_w, value_w, out_w, cotangent)
    ]
    operands.insert(2, owner.T)
    return pl.pallas_call(
        functools.partial(kernel, cores, nz, nx, ny, spans),
        out_shape=(
            jax.ShapeDtypeStruct((tok, cols), BF16),
            jax.ShapeDtypeStruct((wide // n_dp, proj), F32),
        ),
        in_specs=[any_, any_, pl.BlockSpec(memory_space=pltpu.SMEM), any_, any_, any_, any_, any_],
        out_specs=(vmem, vmem),
        scratch_shapes=scratch,
        compiler_params=pltpu.CompilerParams(
            collective_id=0, has_side_effects=True, vmem_limit_bytes=48 * 2**20
        ),
        cost_estimate=pl.CostEstimate(flops=3 * 10**9, bytes_accessed=8 * 2**20, transcendentals=163840),
    )(*operands)


def solution(mesh):
    sizes = (2, mesh.shape["dp"] // 2, mesh.shape["ctx"], mesh.shape["enc"])
    in_specs = (
        P(("dp", "ctx"), None),
        P(("dp", "ctx", "enc"), None, None),
        P(("dp", "ctx"), None),
        P("dp", "enc"),
        P("dp", "enc"),
        P("dp", "enc"),
        P("dp", "enc"),
        P(("dp", "ctx"), "enc"),
    )
    out_specs = (P(("dp", "ctx"), "enc"), P("dp", "enc"))
    return jax.shard_map(
        functools.partial(shards, sizes),
        mesh=mesh,
        in_specs=in_specs,
        out_specs=out_specs,
        check_vma=False,
    )
```

time: 111 us -> 92.3 us (0.83)
  Pallas kernels: 100 us -> 89.4 us
  local copies, waits for them, and re-layouts: 9.11 us -> 2.08 us
    pallas_call x1, Pallas kernels: 100 us -> 89.4 us  [shards(): pl.pallas_call(functools.partial(kernel, cores, nz, nx, ny, spans), out_s...]
    unnamed x17 -> x4, local copies, waits for them, and re-layouts: 9.11 us -> 2.08 us
where the time goes in v2:
time: 92.3 us; the launch traced here: 92.2 us
  Pallas kernels  89.4 us (97%)
  local copies, waits for them, and re-layouts  2.08 us (2%)
    pallas_call x1, Pallas kernels, shards(): pl.pallas_call(functools.partial(kernel, cores, nz, nx, ny, spans), out_s...  89.4 us
    unnamed x4, local copies, waits for them, and re-layouts  2.08 us

profile of v2, /device:TPU:16, one launch (start us, length us, event | category | flops | bytes accessed | tf_op | source)
XLA Modules:
  0.0 92.2 jit_solution(6465281936062646104)
XLA Ops:
  0.6 0.0 copy-start
  0.6 0.7 copy-done
  1.3 89.4 %shard_map.95 = (bf16[256,512]{1,0:T(8,128)(2,1)S(1)}, f32[256,256]{1,0:T(8,128)S(1)}) custom-call(bf16[256,4096]{1,0:T(8,128)(2,1)} %hid_h.1, bf16[3,128,896]{2,1,0:T(8,128)(2,1)} %st_h.1, s32[2,4]{1,0:T(2,128)S(1)} %bitcast.1, bf16[256,256]{1,0:T(8,128)(2,1)} %wq_h.1, bf16[56,256]{1,0:T(8,128)(2,1)} %wk_h.1, bf16[56,256]{1,0:T(8,128)(2,1)} %wv_h.1, ...), custom_call_target="tpu_custom_call" | custom-call | flops 3000000000 | bytes 8388608 | tf_op jit(solution)/shard_map/pallas_call | solution.py:619
  90.7 0.7 copy.12
  91.5 0.7 copy.13
Async XLA Ops:
  0.6 0.7 copy-start

commit v3 on v2

--- a/solution.py
+++ b/solution.py
@@ -69,8 +69,8 @@
 
 
 def kernel(
-    cores, nz, nx, ny, spans, hid_h, st_h, owner, wq_h, wk_h, wv_h, wo_h, cot_h, mixed_o, grad_o,
-    hid, cot, wk_v, wv_v, wq, wo, wkv, kvw_f, kvw, a2a, picked, kv, gpart, rs_out, rs_in, qpad, gpad, probs,
+    cores, nz, nx, ny, spans, hid_h, st_h, owner_h, wq_h, wk_h, wv_h, wo_h, cot_h, mixed_o, grad_o,
+    owner, hid, cot, wk_v, wv_v, wq, wo, wkv, kvw_f, kvw, a2a_0, a2a_1, picked, kv, gpart, rs_out, rs_in, qpad, gpad, probs,
     apad, att, gqpad, ht, hx, gq, part, sib_out, sib_in, zs, z_in, fin, acc,
     local_sem, a2a_s, a2a_r, pick_s, pick_r, rs_s, rs_r, att_s, att_r,
     wo_s, wo_r, wq_s, wq_r, kw_s, kw_r, wo_cs, wo_cr, wq_cs, wq_cr, kw_cs, kw_cr, wq_xs, wq_xr,
@@ -121,6 +121,13 @@
             sent.append(copy)
         return copy
 
+    enc_d = st_h.shape[2]
+    a2a = (a2a_0, a2a_1)
+    lanes = (slice(0, a2a_0.shape[3]), slice(a2a_0.shape[3], enc_d))
+
+    def lane(c):
+        return pl.ds(lanes[c].start, lanes[c].stop - lanes[c].start)
+
     with jax.named_scope("entry"):
         barrier = pltpu.get_barrier_semaphore()
         peers = [sib]
@@ -131,13 +138,19 @@
             pl.semaphore_signal(barrier, inc=1, device_id=peer, device_id_type=MESH)
 
         local = [
-            pltpu.make_async_copy(st_h.at[:, pl.ds(pl.multiple_of(y * piece, 16), piece), :], a2a.at[y], local_sem.at[0]),
+            pltpu.make_async_copy(
+                st_h.at[:, pl.ds(pl.multiple_of(y * piece, 16), piece), lane(0)], a2a_0.at[y], local_sem.at[0]
+            ),
             pltpu.make_async_copy(wo_h, rows_of(wo, dp, wo_h.shape[0]), local_sem.at[1]),
             pltpu.make_async_copy(wq_h, wq.at[z, core], local_sem.at[2]),
             pltpu.make_async_copy(cot_h, cot, local_sem.at[3]),
             pltpu.make_async_copy(hid_h, hid, local_sem.at[4]),
             pltpu.make_async_copy(wk_h, wk_v, local_sem.at[5]),
             pltpu.make_async_copy(wv_h, wv_v, local_sem.at[6]),
+            pltpu.make_async_copy(owner_h, owner, local_sem.at[7]),
+            pltpu.make_async_copy(
+                st_h.at[:, pl.ds(pl.multiple_of(y * piece, 16), piece), lane(1)], a2a_1.at[y], local_sem.at[8]
+            ),
         ]
         for copy in local:
             copy.start()
@@ -226,13 +239,17 @@
         block = wq.at[:, 1 - core]
         remote(block, block, wq_cs, wq_cr, sib, start=False).wait_recv()
 
+    far_first = sorted(range(1, ny), key=lambda k: -min(k, ny - k))
+
+    def spread(c):
+        for k in far_first:
+            to = pl.ds(pl.multiple_of(yat(k) * piece, 16), piece)
+            remote(
+                st_h.at[:, to, lane(c)], a2a[c].at[y], a2a_s.at[c, k - 1], a2a_r.at[c, k - 1], ydev(k)
+            )
+
     with jax.named_scope("spread"):
-        for k in sorted(range(1, ny), key=lambda k: -min(k, ny - k)):
-            to = yat(k)
-            remote(
-                st_h.at[:, pl.ds(pl.multiple_of(to * piece, 16), piece), :],
-                a2a.at[y], a2a_s.at[k - 1], a2a_r.at[k - 1], ydev(k),
-            )
+        spread(0)
     with jax.named_scope("weights_0"):
         out_w.start()
         kv_w.start()
@@ -244,103 +261,108 @@
         for j in range(1, nx):
             part_x = pl.ds(pl.multiple_of(xat(j) * quarter, 16), quarter)
             remote(ht.at[:, :, part_x], hx.at[x], hx_s.at[j - 1], hx_r.at[j - 1], xdev(j))
+    with jax.named_scope("spread_1"):
+        spread(1)
+
+    def weights_step(step):
+        out_w.wait(step)
+        kv_w.wait(step)
+        query_wait(step)
+
     with jax.named_scope("weights_1"):
-        for step in (1, 2):
-            out_w.wait(step)
-            kv_w.wait(step)
-            query_wait(step)
+        weights_step(1)
 
     chunks = 2
     share = tok // chunks
 
-    def rs_move(chunk, way, step):
-        lo, rows = chunk * share, share
-        src = rs_out.at[way, step - 1, pl.ds(lo, rows)]
+    half = tok // 2
+
+    def rs_move(h, way, step):
+        src, dst = rs_out.at[way, step - 1, h], rs_in.at[way, step - 1, h]
         if step == 1:
-            rows = share // 2
-            lo += way * rows
-            src = gpart.at[hy, pl.ds(lo, rows)]
-        dst = rs_in.at[way, step - 1, pl.ds(lo, rows)]
-        return src, dst, rs_s.at[chunk, way, step - 1], rs_r.at[chunk, way, step - 1]
-
-    def rs_start(chunk, step):
+            rows = pl.ds(way * half, half)
+            src, dst = gpart.at[hy, h, rows], dst.at[rows]
+        return src, dst, rs_s.at[h, way, step - 1], rs_r.at[h, way, step - 1]
+
+    def rs_start(h, step):
         for way, to in ((0, ydev(1)), (1, ydev(-1))):
-            remote(*rs_move(chunk, way, step), to)
-
-    def rs_wait(chunk, step):
+            remote(*rs_move(h, way, step), to)
+
+    def rs_wait(h, step):
         for way in range(2):
-            _, dst, s, r = rs_move(chunk, way, step)
+            _, dst, s, r = rs_move(h, way, step)
             remote(dst, dst, s, r, ydev(1), start=False).wait_recv()
 
     def rs_step(step):
         left = hy - step
-        for chunk in range(chunks):
-            rs_wait(chunk, step)
+        for h in range(heads):
+            rs_wait(h, step)
             for way, k in ((0, left), (1, ny - left)):
-                lo, hi = chunk * share, (chunk + 1) * share
+                rows = slice(0, tok)
                 if step == 1:
-                    half = share // 2
-                    other = lo + (1 - way) * half
-                    rs_out[way, step, other : other + half] = gpart[k, other : other + half]
-                    lo += way * half
-                    hi = lo + half
-                rs_out[way, step, lo:hi] = (
-                    rs_in[way, step - 1, lo:hi].astype(F32) + gpart[k, lo:hi].astype(F32)
+                    rows, other = slice(way * half, (way + 1) * half), slice((1 - way) * half, (2 - way) * half)
+                    rs_out[way, step, h, other] = gpart[k, h, other]
+                rs_out[way, step, h, rows] = (
+                    rs_in[way, step - 1, h, rows].astype(F32) + gpart[k, h, rows].astype(F32)
                 ).astype(BF16)
-            rs_start(chunk, step + 1)
-
-    part_rows = pairs // chunks
-
-    def pick_slot(chunk):
-        return lambda k: picked.at[yat(k), pl.ds(chunk * part_rows, part_rows)]
-
-    order = tuple(reversed(range(chunks)))
-    pick_rings = {
-        c: Ring(pick_slot(c), part_rows // 2, pick_s.at[c], pick_r.at[c], ydev(1), ydev(-1)) for c in order
-    }
-
-    def pick_start(step):
-        for c in order:
-            pick_rings[c].start(step, hy)
-
-    def pick_wait(step):
-        for c in order:
-            pick_rings[c].wait(step, hy)
-            if step < hy:
-                pick_rings[c].start(step + 1, hy)
-
-    with jax.named_scope("select"):
+            rs_start(h, step + 1)
+
+    def pick_slot(c):
+        return lambda k: picked.at[yat(k), :, lane(c)]
+
+    pick_rings = [Ring(pick_slot(c), pairs // 2, pick_s.at[c], pick_r.at[c], ydev(1), ydev(-1)) for c in range(2)]
+
+    def pick_wait(c, step):
+        pick_rings[c].wait(step, hy)
+        if step < hy:
+            pick_rings[c].start(step + 1, hy)
+
+    def select(c):
         for k in range(1, ny):
-            block = a2a.at[yat(-k)]
-            remote(block, block, a2a_s.at[k - 1], a2a_r.at[k - 1], ydev(k), start=False).wait_recv()
-        local[0].wait()
+            block = a2a[c].at[yat(-k)]
+            remote(block, block, a2a_s.at[c, k - 1], a2a_r.at[c, k - 1], ydev(k), start=False).wait_recv()
+        if c == 0:
+            local[0].wait()
+            local[7].wait()
+        else:
+            local[8].wait()
         names = [owner[i % owner.shape[0], i // owner.shape[0]] for i in range(used)]
         for i in range(used):
             rank = sum([(names[i] == names[j]).astype(jnp.int32) for j in range(i)], jnp.int32(0))
-            rank = jnp.minimum(rank, a2a.shape[1] - 1)
-            picked[y, i * piece : (i + 1) * piece, :] = a2a[names[i], rank]
-    with jax.named_scope("picked_0"):
-        pick_start(1)
+            rank = jnp.minimum(rank, a2a_0.shape[1] - 1)
+            picked[y, i * piece : (i + 1) * piece, lanes[c]] = a2a[c][names[i], rank]
+
+    with jax.named_scope("select"):
+        select(0)
+        pick_rings[0].start(1, hy)
     with jax.named_scope("weights_2"):
-        out_w.wait(3)
-        out_w.wait(4)
+        weights_step(2)
+    with jax.named_scope("picked_1"):
+        pick_wait(0, 1)
+    with jax.named_scope("select_1"):
+        select(1)
+        pick_rings[1].start(1, hy)
+    with jax.named_scope("weights_3"):
+        weights_step(3)
+    with jax.named_scope("picked_2"):
+        pick_wait(0, 2)
+    with jax.named_scope("weights_4"):
+        weights_step(4)
         local[1].wait()
         out_w.from_sibling()
     with jax.named_scope("grad_partial"):
         local[3].wait()
         for k in range(ny):
             rows = rows_of(wo, yat(hy - k), proj)
-            gpart[(hy - k) % ny] = dot(cot[...], rows[...], NT).astype(BF16)
+            made = dot(cot[...], rows[...], NT).astype(BF16)
+            for h in range(heads):
+                gpart[(hy - k) % ny, h] = made[:, h * HEAD_DIM : (h + 1) * HEAD_DIM]
     with jax.named_scope("rs_1"):
-        for chunk in range(chunks):
-            rs_start(chunk, 1)
-    with jax.named_scope("picked_1"):
-        pick_wait(1)
-    with jax.named_scope("weights_3"):
-        kv_w.wait(3)
-        query_wait(3)
-        kv_w.wait(4)
-        query_wait(4)
+        for h in range(heads):
+            rs_start(h, 1)
+    with jax.named_scope("picked_3"):
+        pick_wait(1, 1)
+    with jax.named_scope("weights_5"):
         kv_w.from_sibling()
     with jax.named_scope("unpack"):
         for i in range(cores * nz):
@@ -352,38 +374,38 @@
     per_span = pairs // spans
 
     def project(ks):
-        for chunk in order:
-            rows = slice(chunk * part_rows, (chunk + 1) * part_rows)
-            made = dot(jnp.concatenate([picked[yat(k), rows, :] for k in ks], axis=0), kvw[...]).astype(BF16)
-            for n, k in enumerate(ks):
-                at = pl.ds(pl.multiple_of(yat(k) * per_span, 16), per_span)
-                for u in range(spans // chunks):
-                    lo = n * part_rows + u * per_span
-                    kv[1 + chunk * (spans // chunks) + u, at, :] = made[lo : lo + per_span]
-                if chunk == chunks - 1:
-                    remote(kv.at[spans, at], kv.at[0, at], halo_s.at[k % ny], halo_r.at[k % ny], xdev(1))
-
+        made = dot(jnp.concatenate([picked[yat(k)] for k in ks], axis=0), kvw[...]).astype(BF16)
+        for n, k in enumerate(ks):
+            at = pl.ds(pl.multiple_of(yat(k) * per_span, 16), per_span)
+            for u in range(spans):
+                lo = n * pairs + u * per_span
+                kv[1 + u, at, :] = made[lo : lo + per_span]
+            remote(kv.at[spans, at], kv.at[0, at], halo_s.at[k % ny], halo_r.at[k % ny], xdev(1))
+
+    with jax.named_scope("picked_4"):
+        pick_wait(0, 3)
     with jax.named_scope("project_1"):
-        project((0, 1))
-    with jax.named_scope("picked_2"):
-        pick_wait(2)
+        project((0, 1, -1))
+    with jax.named_scope("picked_5"):
+        pick_wait(1, 2)
     with jax.named_scope("rs_2"):
         rs_step(1)
     with jax.named_scope("project_2"):
-        project((-1, 2))
-    with jax.named_scope("picked_3"):
-        pick_wait(3)
-    with jax.named_scope("rs_3"):
-        rs_step(2)
-    with jax.named_scope("weights_5"):
+        project((2, -2))
+    with jax.named_scope("weights_6"):
         query_all()
         query_from_sibling()
     with jax.named_scope("queries"):
         qpad[pl.ds(1, tok), :] = dot(hid[...], wq[...].reshape(hid.shape[1], proj)).astype(BF16).astype(F32)
+    with jax.named_scope("picked_6"):
+        pick_wait(0, 4)
+        pick_wait(1, 3)
+    with jax.named_scope("rs_3"):
+        rs_step(2)
     with jax.named_scope("project_3"):
-        project((-2, 3, -3))
-    with jax.named_scope("picked_4"):
-        pick_wait(4)
+        project((3, -3))
+    with jax.named_scope("picked_7"):
+        pick_wait(1, 4)
         project((4,))
     with jax.named_scope("rs_4"):
         rs_step(3)
@@ -428,12 +450,6 @@
         att[y] = apad[pl.ds(1, tok), :].astype(BF16)
         for ring in att_rings:
             ring.start(1, hy)
-    with jax.named_scope("rs_last"):
-        for chunk in range(chunks):
-            rs_wait(chunk, hy)
-        total = gpart[0].astype(F32) + rs_in[0, hy - 1].astype(F32) + rs_in[1, hy - 1].astype(F32)
-        gpad[pl.ds(1, tok), :] = total.astype(BF16).astype(F32)
-
     def backward(g, h):
         rows = pl.ds(g * span, span)
         cols = pl.ds(h * HEAD_DIM, HEAD_DIM)
@@ -459,6 +475,9 @@
 
     with jax.named_scope("backward"):
         for h in range(heads):
+            rs_wait(h, hy)
+            total = gpart[0, h].astype(F32) + rs_in[0, hy - 1, h].astype(F32) + rs_in[1, hy - 1, h].astype(F32)
+            gpad[pl.ds(1, tok), pl.ds(h * HEAD_DIM, HEAD_DIM)] = total.astype(BF16).astype(F32)
             for g in range(spans + 1):
                 backward(g, h)
             gq[h, x] = gqpad[pl.ds(1, tok), pl.ds(h * HEAD_DIM, HEAD_DIM)].astype(BF16)
@@ -539,7 +558,7 @@
             grad_o[:, pl.ds(h * HEAD_DIM, HEAD_DIM)] = fin[h].astype(F32).reshape(wide, HEAD_DIM)
     with jax.named_scope("drain"):
         for copy in sent + [
-            c for ring in (*out_w.rings, *kv_w.rings, query_ring, *pick_rings.values(), *att_rings) for c in ring.sent
+            c for ring in (*out_w.rings, *kv_w.rings, query_ring, *pick_rings, *att_rings) for c in ring.sent
         ]:
             copy.wait_send()
 
@@ -563,6 +582,7 @@
     block = wide // n_dp
     quarter = block // nx
     scratch = [
+        pltpu.SMEM((per, spans), jnp.int32),
         pltpu.VMEM((tok, wide), BF16),
         pltpu.VMEM((tok, cols), BF16),
         pltpu.VMEM(key_w.shape, BF16),
@@ -572,12 +592,13 @@
         pltpu.VMEM((2 * enc_d, proj), BF16),
         pltpu.VMEM((enc_d, 2 * proj), F32),
         pltpu.VMEM((enc_d, 2 * proj), BF16),
-        pltpu.VMEM((ny, slots, piece, enc_d), BF16),
+        pltpu.VMEM((ny, slots, piece, enc_d // 256 * 128 + 128), BF16),
+        pltpu.VMEM((ny, slots, piece, enc_d - enc_d // 256 * 128 - 128), BF16),
         pltpu.VMEM((ny, pairs, enc_d), BF16),
         pltpu.VMEM((spans + 1, keys, 2 * proj), BF16),
-        pltpu.VMEM((ny, tok, proj), BF16),
-        pltpu.VMEM((2, ny // 2, tok, proj), BF16),
-        pltpu.VMEM((2, ny // 2, tok, proj), BF16),
+        pltpu.VMEM((ny, heads, tok, HEAD_DIM), BF16),
+        pltpu.VMEM((2, ny // 2, heads, tok, HEAD_DIM), BF16),
+        pltpu.VMEM((2, ny // 2, heads, tok, HEAD_DIM), BF16),
         pltpu.VMEM((padded, proj), F32),
         pltpu.VMEM((padded, proj), F32),
         pltpu.VMEM(((spans + 1) * heads, tok // spans, keys), F32),
@@ -594,8 +615,8 @@
         pltpu.VMEM((heads, nz - 1, quarter, HEAD_DIM), BF16),
         pltpu.VMEM((heads, nx, quarter, HEAD_DIM), BF16),
         pltpu.VMEM((tok, cols), F32),
-        dma((7,)),
-        dma((ny - 1,)), dma((ny - 1,)),
+        dma((9,)),
+        dma((2, ny - 1)), dma((2, ny - 1)),
         dma((2, 2, ny // 2)), dma((2, 2, ny // 2)),
         dma((2, 2, ny // 2)), dma((2, 2, ny // 2)),
         dma((2, 2, ny // 2)), dma((2, 2, ny // 2)),
@@ -613,16 +634,15 @@
     ]
     operands = [
         pltpu.with_memory_space_constraint(a, pltpu.HBM)
-        for a in (hidden, states, query_w, key_w, value_w, out_w, cotangent)
+        for a in (hidden, states, owner.T, query_w, key_w, value_w, out_w, cotangent)
     ]
-    operands.insert(2, owner.T)
     return pl.pallas_call(
         functools.partial(kernel, cores, nz, nx, ny, spans),
         out_shape=(
             jax.ShapeDtypeStruct((tok, cols), BF16),
             jax.ShapeDtypeStruct((wide // n_dp, proj), F32),
         ),
-        in_specs=[any_, any_, pl.BlockSpec(memory_space=pltpu.SMEM), any_, any_, any_, any_, any_],
+        in_specs=[any_, any_, any_, any_, any_, any_, any_, any_],
         out_specs=(vmem, vmem),
         scratch_shapes=scratch,
         compiler_params=pltpu.CompilerParams(

time: 92.3 us -> 90.3 us (0.978)
  the two profiles are of different devices: /device:TPU:16 before, /device:TPU:4 now
where the time goes in v3:
time: 90.3 us; the launch traced here: 90.1 us
  Pallas kernels  88.1 us (98%)
  local copies, waits for them, and re-layouts  1.41 us (2%)
    pallas_call x1, Pallas kernels, shards(): pl.pallas_call(functools.partial(kernel, cores, nz, nx, ny, spans), out_s...  88.1 us

profile of v3, /device:TPU:4, one launch (start us, length us, event | category | flops | bytes accessed | tf_op | source)
XLA Modules:
  0.0 90.1 jit_solution(3174948844263904720)
XLA Ops:
  0.6 88.1 %shard_map.95 = (bf16[256,512]{1,0:T(8,128)(2,1)S(1)}, f32[256,256]{1,0:T(8,128)S(1)}) custom-call(bf16[256,4096]{1,0:T(8,128)(2,1)} %hid_h.1, bf16[3,128,896]{2,1,0:T(8,128)(2,1)} %st_h.1, s32[2,4]{1,0:T(2,128)} %bitcast.1, bf16[256,256]{1,0:T(8,128)(2,1)} %wq_h.1, bf16[56,256]{1,0:T(8,128)(2,1)} %wk_h.1, bf16[56,256]{1,0:T(8,128)(2,1)} %wv_h.1, ...), custom_call_target="tpu_custom_call" | custom-call | flops 3000000000 | bytes 8388608 | tf_op jit(solution)/shard_map/pallas_call | solution.py:639
  88.7 0.7 copy.12
  89.4 0.7 copy.13

commit v4 on v3

--- a/solution.py
+++ b/solution.py
@@ -382,16 +382,18 @@
                 kv[1 + u, at, :] = made[lo : lo + per_span]
             remote(kv.at[spans, at], kv.at[0, at], halo_s.at[k % ny], halo_r.at[k % ny], xdev(1))
 
+    with jax.named_scope("rs_2"):
+        rs_step(1)
     with jax.named_scope("picked_4"):
         pick_wait(0, 3)
     with jax.named_scope("project_1"):
         project((0, 1, -1))
     with jax.named_scope("picked_5"):
         pick_wait(1, 2)
-    with jax.named_scope("rs_2"):
-        rs_step(1)
     with jax.named_scope("project_2"):
         project((2, -2))
+    with jax.named_scope("rs_3"):
+        rs_step(2)
     with jax.named_scope("weights_6"):
         query_all()
         query_from_sibling()
@@ -400,8 +402,6 @@
     with jax.named_scope("picked_6"):
         pick_wait(0, 4)
         pick_wait(1, 3)
-    with jax.named_scope("rs_3"):
-        rs_step(2)
     with jax.named_scope("project_3"):
         project((3, -3))
     with jax.named_scope("picked_7"):
@@ -542,6 +542,8 @@
         att_wait(3)
     with jax.named_scope("to_z_1"):
         to_z(1)
+    with jax.named_scope("from_z_0"):
+        from_z(0)
     with jax.named_scope("mixed"):
         for k in (0, 1, -1, 2, -2, 3, -3):
             mix(k)
@@ -549,13 +551,13 @@
         mix(4)
         mixed_o[...] = acc[...].astype(BF16)
     with jax.named_scope("from_z"):
-        for h in range(heads):
+        for h in range(1, heads):
             from_z(h)
     with jax.named_scope("from_x"):
         for h in range(heads):
             for j in range(1, nx):
                 f_copy(h, j, False).wait_recv()
-            grad_o[:, pl.ds(h * HEAD_DIM, HEAD_DIM)] = fin[h].astype(F32).reshape(wide, HEAD_DIM)
+            grad_o[:, pl.ds(h * HEAD_DIM, HEAD_DIM)] = fin[h].reshape(wide, HEAD_DIM)
     with jax.named_scope("drain"):
         for copy in sent + [
             c for ring in (*out_w.rings, *kv_w.rings, query_ring, *pick_rings, *att_rings) for c in ring.sent
@@ -636,11 +638,11 @@
         pltpu.with_memory_space_constraint(a, pltpu.HBM)
         for a in (hidden, states, owner.T, query_w, key_w, value_w, out_w, cotangent)
     ]
-    return pl.pallas_call(
+    mixed, grad = pl.pallas_call(
         functools.partial(kernel, cores, nz, nx, ny, spans),
         out_shape=(
             jax.ShapeDtypeStruct((tok, cols), BF16),
-            jax.ShapeDtypeStruct((wide // n_dp, proj), F32),
+            jax.ShapeDtypeStruct((wide // n_dp, proj), BF16),
         ),
         in_specs=[any_, any_, any_, any_, any_, any_, any_, any_],
         out_specs=(vmem, vmem),
@@ -650,6 +652,7 @@
         ),
         cost_estimate=pl.CostEstimate(flops=3 * 10**9, bytes_accessed=8 * 2**20, transcendentals=163840),
     )(*operands)
+    return mixed, grad.astype(F32)
 
 
 def solution(mesh):

time: 90.3 us -> 90.1 us (level)
  the two profiles are of different devices: /device:TPU:4 before, /device:TPU:8 now
where the time goes in v4:
time: 90.1 us; the launch traced here: 89.9 us
  Pallas kernels  87.9 us (98%)
    pallas_call x1, Pallas kernels, shards(): pl.pallas_call(functools.partial(kernel, cores, nz, nx, ny, spans), out_s...  87.9 us

profile of v4, /device:TPU:8, one launch (start us, length us, event | category | flops | bytes accessed | tf_op | source)
XLA Modules:
  0.0 89.9 jit_solution(11983073723015298962)
XLA Ops:
  0.6 87.9 %shard_map.95 = (bf16[256,512]{1,0:T(8,128)(2,1)S(1)}, bf16[256,256]{1,0:T(8,128)(2,1)S(1)}) custom-call(bf16[256,4096]{1,0:T(8,128)(2,1)} %hid_h.1, bf16[3,128,896]{2,1,0:T(8,128)(2,1)} %st_h.1, s32[2,4]{1,0:T(2,128)} %bitcast.1, bf16[256,256]{1,0:T(8,128)(2,1)} %wq_h.1, bf16[56,256]{1,0:T(8,128)(2,1)} %wk_h.1, bf16[56,256]{1,0:T(8,128)(2,1)} %wv_h.1, ...), custom_call_target="tpu_custom_call" | custom-call | flops 3000000000 | bytes 8388608 | tf_op jit(solution)/shard_map/pallas_call | solution.py:641
  88.5 0.7 convert_element_type.3
  89.2 0.7 copy.11
